TPU v7x, 128 devices: a whole 4x4x4 slice. The times are simulated.
128 devices in a mesh: seq: 8 (over y, core), head: 16 (over x, z).
Axes of the slice: x: 4, y: 4, z: 4, core: 2. Of those that a mesh axis runs over, the one named last changes fastest.
Arguments:
- light_query: bfloat16 [8192, 8192], P(('seq', 'head')), may hold values from -6 to 6
- light_key: bfloat16 [8192, 8192], P(('seq', 'head')), may hold values from -6 to 6
- light_value: bfloat16 [8192, 8192], P(('seq', 'head')), may hold values from -12 to 12
- light_decay: bfloat16 [8192, 64], P(('seq', 'head')), may hold values from -1 to 0, as said below
- light_gain: bfloat16 [8192], P('head'), may hold values from 0.5 to 1.5
- soft_query: bfloat16 [8192, 8192], P(('seq', 'head')), may hold values from -6 to 6
- soft_kv: bfloat16 [8192, 2, 1024], P(('seq', 'head')), may hold values from -6 to 6
- doc_blocks: int32 [8], replicated, may hold values from 1 to 32, 64 in all
Outputs:
- light_out: bfloat16 [8192, 8192], P(('seq', 'head'))
- soft_out: bfloat16 [8192, 8192], P(('seq', 'head'))
Inputs may be any that keep to these rules, and one draw needn't show every extreme that they name: `doc_blocks`: 8 lengths summing to 64; the longest is exactly 32. `light_decay`: never positive.
All inputs are finite; a program needn't handle non-finite values.
Results may differ from a plain program's by a relative error of at most 0.0085.
Values may be sent and summed in bfloat16 or wider, within the bound.
A program may use at most 128 MiB of HBM per device.

v0:
```python
import math

import jax
import jax.numpy as jnp
from jax import lax
from jax.sharding import PartitionSpec as P

BLOCK = 256


highest = lax.Precision.HIGHEST
eps_norm = 1e-06
big_negative = -1e30


def shifted(block, axis, distance):
    devices = range(lax.axis_size(axis))
    route = [(i - distance, i) for i in devices if i - distance in devices]
    return lax.ppermute(block, axis, route)


def doc_index(positions, doc_blocks):
    doc_ends = jnp.cumsum(doc_blocks) * 128
    return jnp.sum((positions[:, None] >= doc_ends[None, :]).astype(jnp.int32), axis=1)


def lightning_scan(query_rows, key_rows, value_rows, decay_rows, doc_ids, prior_doc, head_state):
    length = query_rows.shape[0]
    row_order = jnp.arange(BLOCK)
    causal = row_order[:, None] >= row_order[None, :]

    def one_block(state_carry, block_index):
        block_state, block_prior = state_carry
        offset = block_index * BLOCK
        query_half = lax.dynamic_slice_in_dim(query_rows, offset, BLOCK, 0)
        key_half = lax.dynamic_slice_in_dim(key_rows, offset, BLOCK, 0)
        block_query = query_half.astype(jnp.float32)
        block_key = key_half.astype(jnp.float32)
        block_value = lax.dynamic_slice_in_dim(value_rows, offset, BLOCK, 0).astype(jnp.float32)
        block_decay = lax.dynamic_slice_in_dim(decay_rows, offset, BLOCK, 0)
        block_docs = lax.dynamic_slice_in_dim(doc_ids, offset, BLOCK, 0)
        cumulative = jnp.cumsum(block_decay, axis=0)
        allowed = (causal & (block_docs[:, None] == block_docs[None, :]))[None]
        decay_gap = cumulative.T[:, :, None] - cumulative.T[:, None, :]
        decay_weight = jnp.where(allowed, jnp.exp(jnp.where(allowed, decay_gap, 0.0)), 0.0)
        scores = jnp.einsum(
            "thd,jhd->htj", query_half, key_half, preferred_element_type=jnp.float32
        )
        inner_out = jnp.einsum(
            "htj,jhd->thd", scores * decay_weight, block_value, precision=highest
        )
        carried = (block_docs == block_prior).astype(jnp.float32)
        carried_out = (
            jnp.einsum("thd,hde->the", block_query, block_state, precision=highest)
            * (jnp.exp(cumulative) * carried[:, None])[:, :, None]
        )
        last_doc = block_docs[BLOCK - 1]
        tail_weight = (
            jnp.exp(cumulative[BLOCK - 1][None, :] - cumulative)
            * (block_docs == last_doc).astype(jnp.float32)[:, None]
        )
        keep_old = (last_doc == block_prior).astype(jnp.float32)
        new_state = block_state * (jnp.exp(cumulative[BLOCK - 1]) * keep_old)[
            :, None, None
        ] + jnp.einsum("jhd,jh,jhe->hde", block_key, tail_weight, block_value, precision=highest)
        return ((new_state, last_doc), inner_out + carried_out)

    (final_state, final_doc), outputs = lax.scan(
        one_block, (head_state, prior_doc), jnp.arange(length // BLOCK)
    )
    return (outputs.reshape(query_rows.shape), final_state)


def head_norm(mixed_rows, light_gain):
    mean_square = jnp.mean(mixed_rows * mixed_rows, axis=-1, keepdims=True)
    gain_cols = light_gain.astype(jnp.float32).reshape(1, -1, mixed_rows.shape[-1])
    return (mixed_rows * lax.rsqrt(mean_square + eps_norm) * gain_cols).astype(jnp.bfloat16)


def per_device(
    light_query, light_key, light_value, light_decay, light_gain, soft_query, soft_kv, doc_blocks
):
    seq_count = lax.axis_size("seq")
    seq_rank = lax.axis_index("seq")
    head_ranks = lax.axis_size("head")
    query_rows, key_rows, value_rows, decay_rows = (
        lax.all_to_all(light_query, "head", split_axis=1, concat_axis=0, tiled=True),
        lax.all_to_all(light_key, "head", split_axis=1, concat_axis=0, tiled=True),
        lax.all_to_all(light_value, "head", split_axis=1, concat_axis=0, tiled=True),
        lax.all_to_all(light_decay, "head", split_axis=1, concat_axis=0, tiled=True),
    )
    row_count = query_rows.shape[0]
    head_count = decay_rows.shape[1]
    head_width = query_rows.shape[1] // head_count
    head_shape = (row_count, head_count, head_width)
    shard_start = seq_rank * row_count
    positions = shard_start + jnp.arange(row_count, dtype=jnp.int32)
    doc_ids = doc_index(positions, doc_blocks)
    prior_doc = doc_index(jnp.reshape(shard_start - 1, (1,)), doc_blocks)[0]
    query_float = query_rows.astype(jnp.float32).reshape(head_shape)
    decay_float = decay_rows.astype(jnp.float32)
    zero_state = jnp.zeros((head_count, head_width, head_width), jnp.float32)
    local_out, local_state = lightning_scan(
        query_rows.reshape(head_shape),
        key_rows.reshape(head_shape),
        value_rows.reshape(head_shape),
        decay_float,
        doc_ids,
        prior_doc,
        zero_state,
    )
    cumulative = jnp.cumsum(decay_float, axis=0)
    continues = (doc_ids[row_count - 1] == prior_doc).astype(jnp.float32)
    passing = jnp.exp(cumulative[row_count - 1]) * continues

    def chain_step(step_index, received):
        return shifted(
            (received * passing[:, None, None] + local_state).astype(jnp.bfloat16), "seq", 1
        ).astype(jnp.float32)

    incoming = lax.fori_loop(0, seq_count - 1, chain_step, zero_state)
    use_carry = (doc_ids == prior_doc).astype(jnp.float32)
    carried_out = (
        jnp.einsum("thd,hde->the", query_float, incoming, precision=highest)
        * (jnp.exp(cumulative) * use_carry[:, None])[:, :, None]
    )
    light_local = head_norm(local_out + carried_out, light_gain).reshape(
        row_count, head_count * head_width
    )
    light_out = lax.all_to_all(light_local, "head", split_axis=0, concat_axis=1, tiled=True)
    seq_rows = soft_query.shape[0]
    kv_heads = soft_kv.shape[2] // head_width
    copies = head_ranks // kv_heads
    query_flat = soft_query.reshape(seq_rows, 1, soft_query.shape[1])
    repeated = jnp.broadcast_to(
        soft_kv.reshape(seq_rows, 2, kv_heads, 1, head_width),
        (seq_rows, 2, kv_heads, copies, head_width),
    ).reshape(seq_rows, 2, head_ranks * head_width)
    query_local, kv_local = (
        lax.all_to_all(query_flat, "head", split_axis=2, concat_axis=0, tiled=True),
        lax.all_to_all(repeated, "head", split_axis=2, concat_axis=0, tiled=True),
    )
    query_heads = query_local.reshape(head_shape)
    score_scale = 1.0 / math.sqrt(head_width)
    initial = (
        jnp.full((row_count, head_count), big_negative, jnp.float32),
        jnp.zeros((row_count, head_count), jnp.float32),
        jnp.zeros((row_count, head_count, head_width), jnp.float32),
    )
    kv_piece = lax.all_gather(kv_local, "seq", axis=0, tiled=True)
    piece_rows = kv_piece.shape[0]
    sub_rows = 512

    def sub_block(block_index, inner_carry):
        offset = block_index * sub_rows
        key_block = lax.dynamic_slice_in_dim(kv_piece, offset, sub_rows, 0)
        key_pos = offset + jnp.arange(sub_rows, dtype=jnp.int32)
        key_docs = doc_index(key_pos, doc_blocks)
        row_max, denominator, numerator = inner_carry
        scores = (
            jnp.einsum(
                "thd,kd->thk", query_heads, key_block[:, 0, :], preferred_element_type=jnp.float32
            )
            * score_scale
        )
        allowed = (
            (key_docs[None, :] == doc_ids[:, None]) & (key_pos[None, :] <= positions[:, None])
        )[:, None, :]
        new_max = jnp.maximum(row_max, jnp.max(jnp.where(allowed, scores, big_negative), axis=-1))
        weights = jnp.where(allowed, jnp.exp(scores - new_max[:, :, None]), 0.0)
        rescale = jnp.exp(row_max - new_max)
        product = jnp.einsum(
            "thk,kd->thd",
            weights.astype(jnp.bfloat16),
            key_block[:, 1, :],
            preferred_element_type=jnp.float32,
        )
        return (
            new_max,
            denominator * rescale + jnp.sum(weights, axis=-1),
            numerator * rescale[:, :, None] + product,
        )

    row_max, denominator, numerator = lax.fori_loop(0, piece_rows // sub_rows, sub_block, initial)
    soft_local = (
        (numerator / denominator[:, :, None])
        .astype(jnp.bfloat16)
        .reshape(row_count, head_count * head_width)
    )
    soft_out = lax.all_to_all(soft_local, "head", split_axis=0, concat_axis=1, tiled=True)
    return (light_out, soft_out)


def solution(mesh):
    placed = (
        P(("seq", "head"), None),
        P(("seq", "head"), None),
        P(("seq", "head"), None),
        P(("seq", "head"), None),
        P("head"),
        P(("seq", "head"), None),
        P(("seq", "head"), None, None),
        P(),
    )
    return jax.shard_map(
        per_device,
        mesh=mesh,
        in_specs=placed,
        out_specs=(P(("seq", "head"), None), P(("seq", "head"), None)),
        check_vma=False,
    )
```

profile of v0, /device:TPU:8, one launch (start us, length us, event | category | flops | bytes accessed | tf_op | source)
XLA Modules:
  0.0 531.1 jit_solution(93287918255114811)
XLA Ops:
  8.7 7.9 %all-to-all-start = ((bf16[16,2,128]{2,1,0:T(2,128)(2,1)}), bf16[16,2,128]{2,1,0:T(2,128)(2,1)S(1)}, u32[]{:S(2)}, u32[]{:S(2)}) async-start(bf16[16,2,128]{2,1,0:T(2,128)(2,1)} %reshape.296), calls=%async_computation | async-start | bytes 16384 | tf_op jit(solution)/shard_map/all_to_all | solution.py:90
  20.3 3.7 all-to-all-done
  24.0 3.6 all-to-all-start.5
  28.7 9.8 %all-to-all-done.5 = bf16[16,2,8192]{2,1,0:T(2,128)(2,1)S(1)} async-done(((bf16[16,2,8192]{2,1,0:T(2,128)(2,1)}), bf16[16,2,8192]{2,1,0:T(2,128)(2,1)S(1)}, u32[]{:S(2)}, u32[]{:S(2)}) %all-to-all-start.5) | async-done | bytes 524320 | tf_op jit(solution)/shard_map/all_to_all | solution.py:141
  38.5 3.7 all-to-all-start.3
  43.2 14.0 %all-to-all-done.3 = bf16[64,16,512]{2,0,1:T(8,128)(2,1)S(1)} async-done(((bf16[64,16,512]{2,0,1:T(8,128)(2,1)}), bf16[64,16,512]{2,0,1:T(8,128)(2,1)S(1)}, u32[]{:S(2)}, u32[]{:S(2)}) %all-to-all-start.3) | async-done | bytes 1048608 | tf_op jit(solution)/shard_map/all_to_all | solution.py:87
  57.3 3.8 all-to-all-start.1
  65.1 11.7 %all-to-all-done.1 = bf16[64,16,512]{2,0,1:T(8,128)(2,1)S(1)} async-done(((bf16[64,16,512]{2,0,1:T(8,128)(2,1)}), bf16[64,16,512]{2,0,1:T(8,128)(2,1)S(1)}, u32[]{:S(2)}, u32[]{:S(2)}) %all-to-all-start.1) | async-done | bytes 1048608 | tf_op jit(solution)/shard_map/all_to_all | solution.py:88
  76.9 4.3 all-to-all-start.2
  83.4 9.2 %copy.229 = bf16[64,1,8192]{0,1,2:T(2,128)(2,1)} copy(bf16[64,1,8192]{2,0,1:T(8,128)(2,1)} %bitcast.207) | data formatting | bytes 2097152 | tf_op jit(solution)/shard_map/reshape | solution.py:134
  93.2 45.2 %reduce.8 = bf16[8192,64]{1,0:T(8,128)(2,1)S(1)} reduce(bf16[8192,1,64]{2,1,0:T(2,128)(2,1)} %bitcast.195, bf16[]{:T(256)} %broadcast.240), dimensions={1}, to_apply=%bitcast.132.reduce_sub_computation | reduce | bytes 2097154
  147.8 7.2 %all-to-all-start.6 = ((bf16[16,2,16384]{2,1,0:T(2,128)(2,1)}), bf16[16,2,16384]{2,1,0:T(2,128)(2,1)}, u32[]{:S(2)}, u32[]{:S(2)}) async-start(bf16[16,2,16384]{2,1,0:T(2,128)(2,1)} %reshape.300), calls=%async_computation.6 | async-start | bytes 2097152 | tf_op jit(solution)/shard_map/all_to_all | solution.py:140
  157.1 94.7 %while.46 = (s32[]{:T(128)}, f32[4,128,128]{2,1,0:T(8,128)S(1)}, s32[]{:T(128)}, f32[4,256,4,128]{1,0,3,2:T(4,128)}, s32[4]{0:T(128)S(1)}, /*index=5*/f32[1024,4...) while((s32[]{:T(128)}, f32[4,128,128]{2,1,0:T(8,128)S(1)}, ...), condition=%wide.region_6.7_spmd.clone, body=%wide.region_3.6_spmd.clone.sunk | while | flops 874582016 | bytes 18821932 | solution.py:68
  168.5 12.3 %dynamic_update_slice.6 = f32[4,256,4,128]{1,0,3,2:T(4,128)} dynamic-update-slice(f32[4,256,4,128]{1,0,3,2:T(4,128)} %get-tuple-element.759, f32[1,256,4,128]{1,0,3,2:T(1,128)S(1)} %copy.296, s32[]{:T(128)S(6)} %copy.302, s32[]{:T(128)} %constant.127.clone.1..sunk, s32[]{:T(128)} %constant.127.clone.1..sunk, s32[]{:T(128)} %constant.127.clone.1..sunk) | dynamic-update-slice | bytes 1048580 | tf_op jit(solution)/shard_map/while/body/jit(dynamic_update_index_in_dim)/dynamic_update_slice | solution.py:68
  192.2 12.3 %dynamic_update_slice.6 = f32[4,256,4,128]{1,0,3,2:T(4,128)} dynamic-update-slice(f32[4,256,4,128]{1,0,3,2:T(4,128)} %get-tuple-element.759, f32[1,256,4,128]{1,0,3,2:T(1,128)S(1)} %copy.296, s32[]{:T(128)S(6)} %copy.302, s32[]{:T(128)} %constant.127.clone.1..sunk, s32[]{:T(128)} %constant.127.clone.1..sunk, s32[]{:T(128)} %constant.127.clone.1..sunk) | dynamic-update-slice | bytes 1048580 | tf_op jit(solution)/shard_map/while/body/jit(dynamic_update_index_in_dim)/dynamic_update_slice | solution.py:68
  215.9 12.3 %dynamic_update_slice.6 = f32[4,256,4,128]{1,0,3,2:T(4,128)} dynamic-update-slice(f32[4,256,4,128]{1,0,3,2:T(4,128)} %get-tuple-element.759, f32[1,256,4,128]{1,0,3,2:T(1,128)S(1)} %copy.296, s32[]{:T(128)S(6)} %copy.302, s32[]{:T(128)} %constant.127.clone.1..sunk, s32[]{:T(128)} %constant.127.clone.1..sunk, s32[]{:T(128)} %constant.127.clone.1..sunk) | dynamic-update-slice | bytes 1048580 | tf_op jit(solution)/shard_map/while/body/jit(dynamic_update_index_in_dim)/dynamic_update_slice | solution.py:68
  239.6 12.3 %dynamic_update_slice.6 = f32[4,256,4,128]{1,0,3,2:T(4,128)} dynamic-update-slice(f32[4,256,4,128]{1,0,3,2:T(4,128)} %get-tuple-element.759, f32[1,256,4,128]{1,0,3,2:T(1,128)S(1)} %copy.296, s32[]{:T(128)S(6)} %copy.302, s32[]{:T(128)} %constant.127.clone.1..sunk, s32[]{:T(128)} %constant.127.clone.1..sunk, s32[]{:T(128)} %constant.127.clone.1..sunk) | dynamic-update-slice | bytes 1048580 | tf_op jit(solution)/shard_map/while/body/jit(dynamic_update_index_in_dim)/dynamic_update_slice | solution.py:68
  251.9 3.3 reshape.280
  255.2 45.0 %while.47 = (s32[]{:T(128)}, f32[4,128,128]{2,1,0:T(8,128)S(1)}, f32[4]{0:T(128)S(1)}, f32[4,128,128]{2,1,0:T(8,128)S(1)}, s32[]{:T(128)}, /*index=5*/s32[]{:T(128)}) while((s32[]{:T(128)}, f32[4,128,128]{2,1,0:T(8,128)S(1)}, f32[4]{0:T(128)S(1)}, f32[4,128,128]{2,1,0:T(8,128)S(1)}, s32[]{:T(128)}, /*index=5*/s32[]{:T(128)}) %tuple.114), condition=%wide.region_10.11_spmd.clone, body=%wide.region_9.10_spmd.clone.sunk | while | flops 327683 | bytes 1572999 | solution.py:121
  257.2 4.4 collective-permute-done
  263.7 4.4 collective-permute-done
  270.1 4.4 collective-permute-done
  276.5 4.4 collective-permute-done
  282.9 4.4 collective-permute-done
  289.4 4.4 collective-permute-done
  295.8 4.4 collective-permute-done
  305.3 7.1 %all-to-all-start.4 = ((bf16[16,64,512]{2,1,0:T(8,128)(2,1)}), bf16[16,64,512]{2,1,0:T(8,128)(2,1)S(1)}, u32[]{:S(2)}, u32[]{:S(2)}) async-start(bf16[16,64,512]{2,1,0:T(8,128)(2,1)} %all_to_all.109), calls=%async_computation.4 | async-start | bytes 2097152 | tf_op jit(solution)/shard_map/all_to_all | solution.py:130
  312.5 10.2 %reshape.301 = bf16[8192,1,64]{2,1,0:T(2,128)(2,1)} reshape(bf16[16,2,16384]{2,1,0:T(2,128)(2,1)} %all-to-all-done.6) | data formatting | bytes 2097152
  322.7 8.2 %copy.230 = bf16[64,1,8192]{2,0,1:T(8,128)(2,1)S(1)} copy(bf16[64,1,8192]{0,1,2:T(2,128)(2,1)} %bitcast.196) | data formatting | bytes 2097152 | tf_op jit(solution)/shard_map/all_to_all | solution.py:140
  332.3 163.7 %while.48 = (s32[]{:T(128)}, f32[1024,4]{0,1:T(4,128)S(1)}, f32[1024,4]{0,1:T(4,128)S(1)}, f32[1024,4,128]{2,0,1:T(8,128)}, s32[1,8]{1,0:T(1,128)S(1)}, /*index=...) while((s32[]{:T(128)}, f32[1024,4]{0,1:T(4,128)S(1)}, ...), condition=%wide.region_17.18_spmd.clone, body=%wide.region_13.17_spmd.clone.sunk | while | flops 1099990016 | bytes 49830268 | solution.py:184
  337.3 3.8 fusion.85
  347.6 3.8 fusion.85
  357.8 3.8 fusion.85
  368.0 3.8 fusion.85
  378.2 3.8 fusion.85
  388.5 3.8 fusion.85
  398.7 3.8 fusion.85
  408.9 3.8 fusion.85
  419.1 3.8 fusion.85
  429.4 3.8 fusion.85
  439.6 3.8 fusion.85
  449.8 3.8 fusion.85
  460.1 3.8 fusion.85
  470.3 3.8 fusion.85
  480.5 3.8 fusion.85
  490.7 3.8 fusion.85
  500.0 7.2 %all-to-all-start.7 = ((bf16[16,64,512]{2,1,0:T(8,128)(2,1)}), bf16[16,64,512]{2,1,0:T(8,128)(2,1)S(1)}, u32[]{:S(2)}, u32[]{:S(2)}) async-start(bf16[16,64,512]{2,1,0:T(8,128)(2,1)} %all_to_all.120), calls=%async_computation.7 | async-start | bytes 2097152 | tf_op jit(solution)/shard_map/all_to_all | solution.py:190
  508.2 14.9 %all-to-all-done.7 = bf16[16,64,512]{2,1,0:T(8,128)(2,1)S(1)} async-done(((bf16[16,64,512]{2,1,0:T(8,128)(2,1)}), bf16[16,64,512]{2,1,0:T(8,128)(2,1)S(1)}, u32[]{:S(2)}, u32[]{:S(2)}) %all-to-all-start.7) | async-done | bytes 1048608 | tf_op jit(solution)/shard_map/all_to_all | solution.py:190
  (442 shorter events, 189.2 us)
Async XLA Ops:
  8.7 15.4 %all-to-all-start = ((bf16[16,2,128]{2,1,0:T(2,128)(2,1)}), bf16[16,2,128]{2,1,0:T(2,128)(2,1)S(1)}, u32[]{:S(2)}, u32[]{:S(2)}) async-start(bf16[16,2,128]{2,1,0:T(2,128)(2,1)} %reshape.296), calls=%async_computation | async-start | bytes 16384 | tf_op jit(solution)/shard_map/all_to_all | solution.py:90
  18.0 9.6 %copy-start.7 = (bf16[64,8192]{1,0:T(8,128)(2,1)S(1)}, bf16[64,8192]{1,0:T(8,128)(2,1)}, u32[]{:S(2)}) copy-start(bf16[64,8192]{1,0:T(8,128)(2,1)} %param.14) | copy-start | bytes 3145732
  24.0 14.4 %all-to-all-start.5 = ((bf16[16,2,8192]{2,1,0:T(2,128)(2,1)}), bf16[16,2,8192]{2,1,0:T(2,128)(2,1)S(1)}, u32[]{:S(2)}, u32[]{:S(2)}) async-start(bf16[16,2,8192]{2,1,0:T(2,128)(2,1)} %reshape.298), calls=%async_computation.5 | async-start | bytes 1048576 | tf_op jit(solution)/shard_map/all_to_all | solution.py:141
  28.7 13.4 %copy-start.8 = (bf16[64,8192]{1,0:T(8,128)(2,1)S(1)}, bf16[64,8192]{1,0:T(8,128)(2,1)}, u32[]{:S(2)}) copy-start(bf16[64,8192]{1,0:T(8,128)(2,1)} %param.15) | copy-start | bytes 3145732
  38.5 18.8 %all-to-all-start.3 = ((bf16[64,16,512]{2,0,1:T(8,128)(2,1)}), bf16[64,16,512]{2,0,1:T(8,128)(2,1)S(1)}, u32[]{:S(2)}, u32[]{:S(2)}) async-start(bf16[64,16,512]{2,0,1:T(8,128)(2,1)} %bitcast.144), calls=%async_computation.3 | async-start | bytes 2097152 | tf_op jit(solution)/shard_map/all_to_all | solution.py:87
  57.3 6.2 %copy-start.2 = (bf16[64,16,512]{2,0,1:T(8,128)(2,1)}, bf16[64,16,512]{2,0,1:T(8,128)(2,1)S(1)}, u32[]{:S(2)}) copy-start(bf16[64,16,512]{2,0,1:T(8,128)(2,1)S(1)} %all-to-all-done.3) | copy-start | bytes 3145732
  57.3 6.2 %copy-start.10 = (s32[8]{0:T(128)S(1)}, s32[8]{0:T(128)}, u32[]{:S(2)}) copy-start(s32[8]{0:T(128)} %param.21) | copy-start | bytes 100
  57.3 19.6 %all-to-all-start.1 = ((bf16[64,16,512]{2,0,1:T(8,128)(2,1)}), bf16[64,16,512]{2,0,1:T(8,128)(2,1)S(1)}, u32[]{:S(2)}, u32[]{:S(2)}) async-start(bf16[64,16,512]{2,0,1:T(8,128)(2,1)} %bitcast.146), calls=%async_computation.1 | async-start | bytes 2097152 | tf_op jit(solution)/shard_map/all_to_all | solution.py:88
  61.1 20.3 %copy-start.9 = (bf16[512]{0:T(512)(128)(2,1)S(1)}, bf16[512]{0:T(512)(128)(2,1)}, u32[]{:S(2)}) copy-start(bf16[512]{0:T(512)(128)(2,1)} %param.18) | copy-start | bytes 3076
  76.9 15.8 %copy-start.4 = (bf16[64,16,512]{2,0,1:T(8,128)(2,1)}, bf16[64,16,512]{2,0,1:T(8,128)(2,1)S(1)}, u32[]{:S(2)}) copy-start(bf16[64,16,512]{2,0,1:T(8,128)(2,1)S(1)} %all-to-all-done.1) | copy-start | bytes 3145732
  76.9 70.9 %all-to-all-start.2 = ((bf16[64,16,512]{2,0,1:T(8,128)(2,1)}), bf16[64,16,512]{2,0,1:T(8,128)(2,1)}, u32[]{:S(2)}, u32[]{:S(2)}) async-start(bf16[64,16,512]{2,0,1:T(8,128)(2,1)} %bitcast.145), calls=%async_computation.2 | async-start | bytes 2097152 | tf_op jit(solution)/shard_map/all_to_all | solution.py:89
  81.3 251.0 %all-gather.2.cloned.1.call-start = ((), (), s32[]{:S(2)}) async-start(), calls=%async_computation.8 | async-start | bytes 4718592 | tf_op jit(solution)/shard_map/all_gather | solution.py:150
  140.7 4.5 copy-start.3
  147.8 157.6 %all-to-all-start.6 = ((bf16[16,2,16384]{2,1,0:T(2,128)(2,1)}), bf16[16,2,16384]{2,1,0:T(2,128)(2,1)}, u32[]{:S(2)}, u32[]{:S(2)}) async-start(bf16[16,2,16384]{2,1,0:T(2,128)(2,1)} %reshape.300), calls=%async_computation.6 | async-start | bytes 2097152 | tf_op jit(solution)/shard_map/all_to_all | solution.py:140
  157.1 6.2 %copy-start = (bf16[1024,4,128]{2,0,1:T(8,128)(2,1)}, bf16[1024,4,128]{2,0,1:T(8,128)(2,1)S(1)}, u32[]{:S(2)}) copy-start(bf16[1024,4,128]{2,0,1:T(8,128)(2,1)S(1)} %get-tuple-element.780) | copy-start | bytes 3145732 | tf_op jit(solution)/shard_map/while
  168.0 12.9 %copy-start.1 = (bf16[1024,4,128]{2,0,1:T(8,128)(2,1)S(1)}, bf16[1024,4,128]{2,0,1:T(8,128)(2,1)}, u32[]{:S(2)}) copy-start(bf16[1024,4,128]{2,0,1:T(8,128)(2,1)} %copy-done) | copy-start | bytes 3145732 | tf_op jit(solution)/shard_map/while
  180.8 6.2 %copy-start = (bf16[1024,4,128]{2,0,1:T(8,128)(2,1)}, bf16[1024,4,128]{2,0,1:T(8,128)(2,1)S(1)}, u32[]{:S(2)}) copy-start(bf16[1024,4,128]{2,0,1:T(8,128)(2,1)S(1)} %get-tuple-element.780) | copy-start | bytes 3145732 | tf_op jit(solution)/shard_map/while
  191.7 12.9 %copy-start.1 = (bf16[1024,4,128]{2,0,1:T(8,128)(2,1)S(1)}, bf16[1024,4,128]{2,0,1:T(8,128)(2,1)}, u32[]{:S(2)}) copy-start(bf16[1024,4,128]{2,0,1:T(8,128)(2,1)} %copy-done) | copy-start | bytes 3145732 | tf_op jit(solution)/shard_map/while
  204.5 6.2 %copy-start = (bf16[1024,4,128]{2,0,1:T(8,128)(2,1)}, bf16[1024,4,128]{2,0,1:T(8,128)(2,1)S(1)}, u32[]{:S(2)}) copy-start(bf16[1024,4,128]{2,0,1:T(8,128)(2,1)S(1)} %get-tuple-element.780) | copy-start | bytes 3145732 | tf_op jit(solution)/shard_map/while
  215.3 12.9 %copy-start.1 = (bf16[1024,4,128]{2,0,1:T(8,128)(2,1)S(1)}, bf16[1024,4,128]{2,0,1:T(8,128)(2,1)}, u32[]{:S(2)}) copy-start(bf16[1024,4,128]{2,0,1:T(8,128)(2,1)} %copy-done) | copy-start | bytes 3145732 | tf_op jit(solution)/shard_map/while
  228.2 6.2 %copy-start = (bf16[1024,4,128]{2,0,1:T(8,128)(2,1)}, bf16[1024,4,128]{2,0,1:T(8,128)(2,1)S(1)}, u32[]{:S(2)}) copy-start(bf16[1024,4,128]{2,0,1:T(8,128)(2,1)S(1)} %get-tuple-element.780) | copy-start | bytes 3145732 | tf_op jit(solution)/shard_map/while
  239.0 12.9 %copy-start.1 = (bf16[1024,4,128]{2,0,1:T(8,128)(2,1)S(1)}, bf16[1024,4,128]{2,0,1:T(8,128)(2,1)}, u32[]{:S(2)}) copy-start(bf16[1024,4,128]{2,0,1:T(8,128)(2,1)} %copy-done) | copy-start | bytes 3145732 | tf_op jit(solution)/shard_map/while
  255.3 6.3 %collective-permute-start = (bf16[4,128,128]{2,1,0:T(8,128)(2,1)S(1)}, bf16[4,128,128]{2,1,0:T(8,128)(2,1)S(1)}, u32[]{:S(2)}, u32[]{:S(2)}) collective-permute-start(bf16[4,128,128]{2,1,0:T(8,128)(2,1)S(1)} %fusion.79), channel_id=1, source_target_pairs={{0,16},{16,32},{32,48},{48,64},{64,80},{80,96},{96,112},{1,17},{17... | collective-permute-start | bytes 393224 | tf_op jit(solution)/shard_map/while/body/eval_jaxpr/ppermute | solution.py:19
  261.7 6.3 %collective-permute-start = (bf16[4,128,128]{2,1,0:T(8,128)(2,1)S(1)}, bf16[4,128,128]{2,1,0:T(8,128)(2,1)S(1)}, u32[]{:S(2)}, u32[]{:S(2)}) collective-permute-start(bf16[4,128,128]{2,1,0:T(8,128)(2,1)S(1)} %fusion.79), channel_id=1, source_target_pairs={{0,16},{16,32},{32,48},{48,64},{64,80},{80,96},{96,112},{1,17},{17... | collective-permute-start | bytes 393224 | tf_op jit(solution)/shard_map/while/body/eval_jaxpr/ppermute | solution.py:19
  268.2 6.3 %collective-permute-start = (bf16[4,128,128]{2,1,0:T(8,128)(2,1)S(1)}, bf16[4,128,128]{2,1,0:T(8,128)(2,1)S(1)}, u32[]{:S(2)}, u32[]{:S(2)}) collective-permute-start(bf16[4,128,128]{2,1,0:T(8,128)(2,1)S(1)} %fusion.79), channel_id=1, source_target_pairs={{0,16},{16,32},{32,48},{48,64},{64,80},{80,96},{96,112},{1,17},{17... | collective-permute-start | bytes 393224 | tf_op jit(solution)/shard_map/while/body/eval_jaxpr/ppermute | solution.py:19
  274.6 6.3 %collective-permute-start = (bf16[4,128,128]{2,1,0:T(8,128)(2,1)S(1)}, bf16[4,128,128]{2,1,0:T(8,128)(2,1)S(1)}, u32[]{:S(2)}, u32[]{:S(2)}) collective-permute-start(bf16[4,128,128]{2,1,0:T(8,128)(2,1)S(1)} %fusion.79), channel_id=1, source_target_pairs={{0,16},{16,32},{32,48},{48,64},{64,80},{80,96},{96,112},{1,17},{17... | collective-permute-start | bytes 393224 | tf_op jit(solution)/shard_map/while/body/eval_jaxpr/ppermute | solution.py:19
  281.0 6.3 %collective-permute-start = (bf16[4,128,128]{2,1,0:T(8,128)(2,1)S(1)}, bf16[4,128,128]{2,1,0:T(8,128)(2,1)S(1)}, u32[]{:S(2)}, u32[]{:S(2)}) collective-permute-start(bf16[4,128,128]{2,1,0:T(8,128)(2,1)S(1)} %fusion.79), channel_id=1, source_target_pairs={{0,16},{16,32},{32,48},{48,64},{64,80},{80,96},{96,112},{1,17},{17... | collective-permute-start | bytes 393224 | tf_op jit(solution)/shard_map/while/body/eval_jaxpr/ppermute | solution.py:19
  287.4 6.3 %collective-permute-start = (bf16[4,128,128]{2,1,0:T(8,128)(2,1)S(1)}, bf16[4,128,128]{2,1,0:T(8,128)(2,1)S(1)}, u32[]{:S(2)}, u32[]{:S(2)}) collective-permute-start(bf16[4,128,128]{2,1,0:T(8,128)(2,1)S(1)} %fusion.79), channel_id=1, source_target_pairs={{0,16},{16,32},{32,48},{48,64},{64,80},{80,96},{96,112},{1,17},{17... | collective-permute-start | bytes 393224 | tf_op jit(solution)/shard_map/while/body/eval_jaxpr/ppermute | solution.py:19
  293.9 6.3 %collective-permute-start = (bf16[4,128,128]{2,1,0:T(8,128)(2,1)S(1)}, bf16[4,128,128]{2,1,0:T(8,128)(2,1)S(1)}, u32[]{:S(2)}, u32[]{:S(2)}) collective-permute-start(bf16[4,128,128]{2,1,0:T(8,128)(2,1)S(1)} %fusion.79), channel_id=1, source_target_pairs={{0,16},{16,32},{32,48},{48,64},{64,80},{80,96},{96,112},{1,17},{17... | collective-permute-start | bytes 393224 | tf_op jit(solution)/shard_map/while/body/eval_jaxpr/ppermute | solution.py:19
  305.3 194.6 %all-to-all-start.4 = ((bf16[16,64,512]{2,1,0:T(8,128)(2,1)}), bf16[16,64,512]{2,1,0:T(8,128)(2,1)S(1)}, u32[]{:S(2)}, u32[]{:S(2)}) async-start(bf16[16,64,512]{2,1,0:T(8,128)(2,1)} %all_to_all.109), calls=%async_computation.4 | async-start | bytes 2097152 | tf_op jit(solution)/shard_map/all_to_all | solution.py:130
  335.4 1.9 copy-start.5
  341.2 1.3 copy-start.6
  345.6 1.9 copy-start.5
  355.9 1.9 copy-start.5
  366.1 1.9 copy-start.5
  376.3 1.9 copy-start.5
  386.6 1.9 copy-start.5
  396.8 1.9 copy-start.5
  407.0 1.9 copy-start.5
  417.2 1.9 copy-start.5
  427.5 1.9 copy-start.5
  437.7 1.9 copy-start.5
  447.9 1.9 copy-start.5
  458.1 1.9 copy-start.5
  468.4 1.9 copy-start.5
  478.6 1.9 copy-start.5
  488.8 1.9 copy-start.5
  500.0 23.2 %all-to-all-start.7 = ((bf16[16,64,512]{2,1,0:T(8,128)(2,1)}), bf16[16,64,512]{2,1,0:T(8,128)(2,1)S(1)}, u32[]{:S(2)}, u32[]{:S(2)}) async-start(bf16[16,64,512]{2,1,0:T(8,128)(2,1)} %all_to_all.120), calls=%async_computation.7 | async-start | bytes 2097152 | tf_op jit(solution)/shard_map/all_to_all | solution.py:190
  (15 other events, 20.1 us)
Sparse Core Ops, SparseCore 0:
  145.3 32.5 all-gather.1
where the time goes:
time: 536 us; the launch traced here: 531 us
  local copies, waits for them, and re-layouts  145 us (27%)
  matrix products  117 us (22%)
  other arithmetic  100 us (19%)
  waiting for transfers between devices  84.7 us (16%)
  starting transfers between devices  58.2 us (11%)
  between operations  15.7 us (3%)
  loops' own time  10 us (2%)
    dot_general x16, matrix products, sub_block(): jnp.einsum('thk,kd->thd', weights.astype(jnp.bfloat16), key_block[:, 1, :...  61.5 us
    dynamic_update_slice x8, local copies, waits for them, and re-layouts, lightning_scan(): lax.scan(one_block, (head_state, prior_doc), jnp.arange(length // BLOCK))  51.3 us
    unnamed x7, other arithmetic  45.3 us
    dot_general x16, matrix products, sub_block(): jnp.einsum('thd,kd->thk', query_heads, key_block[:, 0, :], preferred_elem...  40.2 us
    ppermute x7, waiting for transfers between devices, shifted(): return lax.ppermute(block, axis, route)  30.5 us
    reduce_sum x16, other arithmetic, sub_block(): jnp.sum(weights, axis=-1)  29.6 us
    while x100, local copies, waits for them, and re-layouts  21.4 us
    unnamed x27, local copies, waits for them, and re-layouts  17.4 us
  transfers between devices with their start and end apart: 16, of which 12 were waited for; matrix products, arithmetic and copies ran while one was open for 63% of the time, Pallas kernels for 0%

commit v1 on v0

v1 whole, which is shorter than its diff:
```python
import functools
import math

import jax
import jax.numpy as jnp
from jax import lax
from jax.experimental import pallas as pl
from jax.experimental.pallas import tpu as pltpu
from jax.sharding import PartitionSpec as P

MESH = pl.DeviceIdType.MESH
F32, BF16 = jnp.float32, jnp.bfloat16
HD = 128
RUN = 256
PIECE = 64
WIDE = 1024
SHARD = 1024
SPAN = 1024
LOG2E = math.log2(math.e)
SCALE = LOG2E / math.sqrt(HD)
NEG = -1e30

KV, DEC, GAIN, LK, LV, LQ, SQ, ST, TOT, IN, LO, SO, ZS, XS, KINDS = range(15)

NT = (((1,), (1,)), ((), ()))
TN = (((0,), (0,)), ((), ()))


def kernel(
    docs_ref, lq_ref, lk_ref, lv_ref, dec_ref, gain_ref, sq_ref, kv_ref,
    lo_ref, so_ref,
    lq, lk, lv, dec_out, dec, gains, inner, lout, part, tot, parts, tots, back, incoming,
    sq, kv, sout, cums, send, recv, z_recv, x_recv,
):
    s = lax.axis_index("seq")
    h = lax.axis_index("head")
    y, c = s // 2, s % 2
    x, z = h // 4, h % 4
    group = c * 4 + z
    member = y * 4 + x

    def yc(d):
        return (s + d) % 8

    def zc(d):
        other = (group + d) % 8
        return other, (y * 2 + other // 4, x * 4 + other % 4)

    def xz(d):
        return (s, (h + d) % 16)

    def xy(d):
        other = (member + d) % 16
        return other, ((other // 4) * 2 + c, (other % 4) * 4 + z)

    def push(kind, src, dst, device, recv_sem=None):
        pltpu.make_async_remote_copy(
            src_ref=src, dst_ref=dst, send_sem=send.at[kind],
            recv_sem=recv.at[kind] if recv_sem is None else recv_sem,
            device_id=device, device_id_type=MESH,
        ).start()

    def keep(kind, src, dst):
        pltpu.make_async_copy(src, dst, recv.at[kind]).start()

    def landed(sem, ref):
        pltpu.make_async_copy(ref, ref, sem).wait()

    def each(n, body):
        def step(d, carry):
            body(d)
            return carry
        lax.fori_loop(1, n, step, 0)

    barrier = pltpu.get_barrier_semaphore()

    def greet(device):
        pl.semaphore_signal(barrier, inc=1, device_id=device, device_id_type=MESH)

    each(8, lambda d: greet((yc(d), h)))
    each(8, lambda d: greet(zc(d)[1]))
    each(16, lambda d: greet(xz(d)))
    each(16, lambda d: greet(xy(d)[1]))
    wide = jnp.concatenate([dec_ref[...], dec_ref[...]], axis=1).astype(F32)
    for g in range(8):
        dec_out[g] = (wide if g == 0 else pltpu.roll(wide, 128 - 8 * g, 1)).astype(BF16)
    pl.semaphore_wait(barrier, 7 + 7 + 15 + 15)

    mine = pl.ds(s * SHARD + h * PIECE, PIECE)

    def send_kv(d):
        to = yc(d)
        push(KV, kv_ref.at[:, pl.ds(to * HD, HD)], kv.at[mine, pl.ds(0, HD)], (to, h))
        push(KV, kv_ref.at[:, pl.ds(WIDE + to * HD, HD)], kv.at[mine, pl.ds(HD, HD)], (to, h))

    each(8, send_kv)
    keep(KV, kv_ref.at[:, pl.ds(s * HD, HD)], kv.at[mine, pl.ds(0, HD)])
    keep(KV, kv_ref.at[:, pl.ds(WIDE + s * HD, HD)], kv.at[mine, pl.ds(HD, HD)])

    rows = pl.ds(z * PIECE, PIECE)

    def send_light(kind, ref, buf):
        def one(d):
            other, device = zc(d)
            push(kind, ref.at[:, pl.ds(other * WIDE, WIDE)], buf.at[c, rows, :], device)
        each(8, one)
        keep(kind, ref.at[:, pl.ds(group * WIDE, WIDE)], buf.at[c, rows, :])

    def send_dec(d):
        other, device = zc(d)
        push(DEC, dec_out.at[other], dec.at[c, rows, :], device)

    each(8, send_dec)
    keep(DEC, dec_out.at[group], dec.at[c, rows, :])
    send_light(LK, lk_ref, lk)
    send_light(LV, lv_ref, lv)

    def send_sq(d):
        to = yc(d)
        push(SQ, sq_ref.at[:, pl.ds(to * WIDE, WIDE)], sq.at[s], (to, h))

    each(8, send_sq)
    keep(SQ, sq_ref.at[:, pl.ds(s * WIDE, WIDE)], sq.at[s])

    landed(recv.at[KV], kv.at[pl.ds(0, 8 * PIECE)])

    def send_z(t, carry):
        part_rows = kv.at[pl.ds(t * SHARD + h * PIECE, PIECE)]
        def one(d):
            push(ZS, part_rows, part_rows, (s, x * 4 + (z + d) % 4), z_recv.at[t])
        each(4, one)
        return carry

    lax.fori_loop(0, 8, send_z, 0)
    send_light(LQ, lq_ref, lq)

    def send_gain(d):
        push(GAIN, gain_ref, gains.at[h], xz(d))

    each(16, send_gain)
    keep(GAIN, gain_ref, gains.at[h])

    def send_x(t, carry):
        landed(z_recv.at[t], kv.at[pl.ds(0, 3 * PIECE)])
        part_rows = kv.at[pl.ds(t * SHARD + x * RUN, RUN)]
        def one(d):
            push(XS, part_rows, part_rows, (s, ((x + d) % 4) * 4 + z), x_recv.at[t])
        each(4, one)
        return carry

    lax.fori_loop(0, 8, send_x, 0)

    ends = []
    total = jnp.int32(0)
    for i in range(8):
        total = total + docs_ref[i] * 128
        ends.append(total)

    def doc_of(pos):
        found = jnp.zeros_like(pos)
        for end in ends:
            found = found + jnp.where(pos >= end, 1, 0)
        return found

    column = lax.broadcasted_iota(jnp.int32, (RUN, 1), 0)
    line = lax.broadcasted_iota(jnp.int32, (1, RUN), 1)
    causal = column >= line
    lower = jnp.where(causal, 1.0, 0.0).astype(BF16)

    def run_start(i):
        return (2 * y + i) * SHARD + x * RUN

    landed(recv.at[DEC], dec)
    landed(recv.at[LK], lk)
    landed(recv.at[LV], lv)

    def add_states(i, carry):
        cum = jnp.dot(lower, dec[i], preferred_element_type=F32)
        cums[i] = cum
        start = run_start(i)
        last = doc_of(start + RUN - 1)
        tail = jnp.exp(cum[RUN - 1:RUN, :] - cum) * jnp.where(doc_of(start + column) == last, 1.0, 0.0)
        tot[i] = jnp.broadcast_to(cum.T[0:8, RUN - 1:RUN], (8, 128))
        for j in range(8):
            cols = pl.ds(j * HD, HD)
            weighted = (lv[i, :, cols].astype(F32) * tail[:, j:j + 1]).astype(BF16)
            added = lax.dot_general(lk[i, :, cols], weighted, TN, preferred_element_type=F32)
            part[i, pl.ds(j * HD, HD), :] = added.astype(BF16)
        return carry

    lax.fori_loop(0, 2, add_states, 0)

    def send_state(d):
        other, device = xy(d)
        push(TOT, tot, tots.at[y, :, x], device)
        push(ST, part.at[:, pl.ds(other * 64, 64), :], parts.at[y, :, x], device)

    each(16, send_state)
    keep(TOT, tot, tots.at[y, :, x])
    keep(ST, part.at[:, pl.ds(member * 64, 64), :], parts.at[y, :, x])

    landed(recv.at[LQ], lq)

    def inner_run(i, carry):
        cum = cums[i]
        across = cum.T
        start = run_start(i)
        allowed = causal & (doc_of(start + column) == doc_of(start + line))
        for j in range(8):
            cols = pl.ds(j * HD, HD)
            gap = cum[:, j:j + 1] - across[j:j + 1, :]
            weight = jnp.exp(jnp.where(allowed, gap, NEG))
            scores = lax.dot_general(lq[i, :, cols], lk[i, :, cols], NT, preferred_element_type=F32)
            inner[i, :, cols] = jnp.dot(
                (scores * weight).astype(BF16), lv[i, :, cols], preferred_element_type=F32
            )
        return carry

    lax.fori_loop(0, 2, inner_run, 0)

    landed(recv.at[TOT], tots)
    landed(recv.at[ST], parts)

    def scan_runs(p, state):
        a, b, e = p // 8, (p // 4) % 2, p % 4
        back[a, b, e] = state.astype(BF16)
        start = p * RUN
        same = jnp.where(doc_of(start + RUN - 1) == doc_of(start - 1), 1.0, 0.0)
        factor = jnp.exp(tots[a, b, e, pl.ds(member // 2, 1), :]) * same
        return state * factor + parts[a, b, e].astype(F32)

    lax.fori_loop(0, 32, scan_runs, jnp.zeros((64, HD), F32))

    def send_back(d):
        other, device = xy(d)
        push(IN, back.at[other // 4, :, other % 4], incoming.at[:, pl.ds(member * 64, 64), :], device)

    each(16, send_back)
    keep(IN, back.at[y, :, x], incoming.at[:, pl.ds(member * 64, 64), :])

    landed(recv.at[SQ], sq)
    token = lax.broadcasted_iota(jnp.int32, (8 * PIECE, 1), 0) % PIECE
    key_line = lax.broadcasted_iota(jnp.int32, (1, SPAN), 1)

    def soft_piece(t, carry):
        landed(x_recv.at[t], kv.at[pl.ds(0, 3 * RUN)])
        first = t * SHARD + h * PIECE
        doc_start = jnp.int32(0)
        for end in ends:
            doc_start = jnp.where(first >= end, end, doc_start)
        query = jnp.concatenate([sq[t, :, pl.ds(j * HD, HD)] for j in range(8)], axis=0)

        def block(k, stats, diagonal):
            top, denominator, acc = stats
            limit = first + PIECE - SPAN * k
            start = pl.multiple_of(jnp.maximum(limit - SPAN, 0), PIECE)
            key_pos = start + key_line
            scores = lax.dot_general(
                query, kv[pl.ds(start, SPAN), pl.ds(0, HD)], NT, preferred_element_type=F32
            )
            if diagonal:
                kept = (key_pos >= doc_start) & (key_pos <= first + token)
                scores = jnp.where(kept, scores, NEG)
            else:
                kept = (key_pos >= doc_start) & (key_pos < limit)
                scores = scores + jnp.where(kept, 0.0, NEG)
            new_top = jnp.max(scores, axis=1, keepdims=True)
            if not diagonal:
                new_top = jnp.maximum(top, new_top)
            weights = jnp.exp2((scores - new_top) * SCALE)
            summed = jnp.sum(weights, axis=1, keepdims=True)
            product = jnp.dot(
                weights.astype(BF16), kv[pl.ds(start, SPAN), pl.ds(HD, HD)],
                preferred_element_type=F32,
            )
            if diagonal:
                return new_top, summed, product
            rescale = jnp.exp2((top - new_top) * SCALE)
            return new_top, denominator * rescale + summed, acc * rescale + product

        stats = block(0, (None, None, None), True)
        top, denominator, acc = lax.fori_loop(
            1, jnp.minimum(t + 1, 4), lambda k, st: block(k, st, False), stats
        )
        result = (acc / denominator).astype(BF16)
        for j in range(8):
            sout[t, :, pl.ds(j * HD, HD)] = result[j * PIECE:(j + 1) * PIECE, :]

        target = so_ref.at[:, pl.ds(s * WIDE, WIDE)]

        @pl.when(t == s)
        def _():
            keep(SO, sout.at[t], target)

        @pl.when(t != s)
        def _():
            push(SO, sout.at[t], target, (t, h))
        return carry

    lax.fori_loop(0, 4, soft_piece, 0)

    landed(recv.at[GAIN], gains)
    landed(recv.at[IN], incoming)

    def finish(i, carry):
        start = run_start(i)
        carried = jnp.where(doc_of(start + column) == doc_of(start - 1), 1.0, 0.0)
        reach = jnp.exp(cums[i]) * carried
        for j in range(8):
            cols = pl.ds(j * HD, HD)
            entering = jnp.dot(
                lq[i, :, cols], incoming[i, pl.ds(j * HD, HD), :], preferred_element_type=F32
            )
            mixed = inner[i, :, cols] + entering * reach[:, j:j + 1]
            mean_square = jnp.mean(mixed * mixed, axis=1, keepdims=True)
            gain = gains[2 * group + j // 4, pl.ds(j % 4, 1), :]
            lout[i, :, cols] = (mixed * lax.rsqrt(mean_square + 1e-6) * gain).astype(BF16)
        return carry

    lax.fori_loop(0, 2, finish, 0)

    target = lo_ref.at[:, pl.ds(group * WIDE, WIDE)]

    def send_out(d):
        other, device = zc(d)
        push(LO, lout.at[other // 4, pl.ds((other % 4) * PIECE, PIECE), :], target, device)

    each(8, send_out)
    keep(LO, lout.at[c, rows, :], target)

    lax.fori_loop(4, 8, soft_piece, 0)

    landed(send.at[KV], kv.at[pl.ds(0, 7 * PIECE)])
    landed(send.at[DEC], dec_out.at[pl.ds(0, 7)])
    landed(send.at[GAIN], gains.at[pl.ds(0, 15)])
    for kind in (LK, LV, LQ, SQ, LO, SO):
        landed(send.at[kind], sq.at[pl.ds(0, 7)])
    landed(send.at[ZS], kv.at[pl.ds(0, 24 * PIECE)])
    landed(send.at[XS], kv.at[pl.ds(0, 24 * RUN)])
    landed(send.at[TOT], inner.at[0, pl.ds(0, 15 * 16), pl.ds(0, HD)])
    landed(send.at[ST], kv.at[pl.ds(0, 15 * 64)])
    landed(send.at[IN], kv.at[pl.ds(0, 15 * 64)])
    landed(recv.at[LO], lo_ref)
    landed(recv.at[SO], so_ref)


def per_device(
    light_query, light_key, light_value, light_decay, light_gain, soft_query, soft_kv, doc_blocks
):
    gain = jnp.pad(light_gain.astype(F32).reshape(4, HD), ((0, 4), (0, 0)))
    kv = soft_kv.reshape(PIECE, 2 * WIDE)
    anywhere = pl.BlockSpec(memory_space=pl.ANY)
    vmem = pl.BlockSpec(memory_space=pltpu.VMEM)
    out = jax.ShapeDtypeStruct((PIECE, 8 * WIDE), BF16)
    scratch = [
        pltpu.VMEM((2, RUN, WIDE), BF16),
        pltpu.VMEM((2, RUN, WIDE), BF16),
        pltpu.VMEM((2, RUN, WIDE), BF16),
        pltpu.VMEM((8, PIECE, 128), BF16),
        pltpu.VMEM((2, RUN, 128), BF16),
        pltpu.VMEM((16, 8, HD), F32),
        pltpu.VMEM((2, RUN, WIDE), F32),
        pltpu.VMEM((2, RUN, WIDE), BF16),
        pltpu.VMEM((2, WIDE, HD), BF16),
        pltpu.VMEM((2, 8, 128), F32),
        pltpu.VMEM((4, 2, 4, 64, HD), BF16),
        pltpu.VMEM((4, 2, 4, 8, 128), F32),
        pltpu.VMEM((4, 2, 4, 64, HD), BF16),
        pltpu.VMEM((2, WIDE, HD), BF16),
        pltpu.VMEM((8, PIECE, WIDE), BF16),
        pltpu.VMEM((8 * SHARD, 2 * HD), BF16),
        pltpu.VMEM((8, PIECE, WIDE), BF16),
        pltpu.VMEM((2, RUN, 128), F32),
        pltpu.SemaphoreType.DMA((KINDS,)),
        pltpu.SemaphoreType.DMA((KINDS,)),
        pltpu.SemaphoreType.DMA((8,)),
        pltpu.SemaphoreType.DMA((8,)),
    ]
    return pl.pallas_call(
        kernel,
        out_shape=(out, out),
        in_specs=[
            pl.BlockSpec(memory_space=pltpu.SMEM), anywhere, anywhere, anywhere, vmem, anywhere,
            anywhere, anywhere,
        ],
        out_specs=(anywhere, anywhere),
        scratch_shapes=scratch,
        compiler_params=pltpu.CompilerParams(
            collective_id=0, has_side_effects=True, vmem_limit_bytes=48 * 2**20
        ),
    )(doc_blocks, light_query, light_key, light_value, light_decay, gain, soft_query, kv)


def solution(mesh):
    placed = (
        P(("seq", "head"), None),
        P(("seq", "head"), None),
        P(("seq", "head"), None),
        P(("seq", "head"), None),
        P("head"),
        P(("seq", "head"), None),
        P(("seq", "head"), None, None),
        P(),
    )
    return jax.shard_map(
        per_device,
        mesh=mesh,
        in_specs=placed,
        out_specs=(P(("seq", "head"), None), P(("seq", "head"), None)),
        check_vma=False,
    )
```

time: 536 us -> 144 us (0.27)
  the two profiles are of different devices: /device:TPU:8 before, /device:TPU:25 now
where the time goes in v1:
time: 144 us; the launch traced here: 143 us
  Pallas kernels  135 us (94%)
  local copies, waits for them, and re-layouts  7.94 us (6%)
    pallas_call x1, Pallas kernels, per_device(): pl.pallas_call(kernel, out_shape=(out, out), in_specs=[pl.BlockSpec(memor...  135 us
    unnamed x15, local copies, waits for them, and re-layouts  7.94 us

profile of v1, /device:TPU:25, one launch (start us, length us, event | category | flops | bytes accessed | tf_op | source)
XLA Modules:
  0.0 143.4 jit_solution(13503230745952509955)
XLA Ops:
  0.6 0.0 copy-start.5
  0.6 0.7 copy-done.5
  1.3 0.0 copy-start.3
  1.3 1.0 copy.10
  2.3 0.0 copy-start.4
  2.3 0.0 copy-done.3
  2.4 0.6 copy-done.4
  3.0 0.0 copy-start
  3.0 1.2 copy-done
  4.2 0.0 copy-start.1
  4.2 1.2 copy-done.1
  5.4 0.0 copy-start.2
  5.4 1.2 copy-done.2
  6.7 134.8 %shard_map.95 = (bf16[64,8192]{1,0:T(8,128)(2,1)S(1)}, bf16[64,8192]{1,0:T(8,128)(2,1)S(1)}) custom-call(s32[8]{0:T(128)S(1)} %copy-done.4, bf16[64,8192]{1,0:T(8,128)(2,1)S(1)} %copy-done, bf16[64,8192]{1,0:T(8,128)(2,1)S(1)} %copy-done.1, bf16[64,8192]{1,0:T(8,128)(2,1)S(1)} %copy-done.2, bf16[64,64]{1,0:T(8,128)(2,1)S(1)} %copy-done.3, ...), custom_call_target="tpu_custom_call" | custom-call | tf_op jit(solution)/shard_map/pallas_call | solution.py:379
  141.4 1.0 copy.13
  142.4 1.0 copy.14
  (1 shorter events, 0.0 us)
Async XLA Ops:
  0.6 0.7 copy-start.5
  1.3 1.0 copy-start.3
  2.3 0.7 copy-start.4
  3.0 1.2 copy-start
  4.2 1.2 copy-start.1
  5.4 1.2 copy-start.2

commit v2 on v1

v2 whole, which is shorter than its diff:
```python
import functools
import math

import jax
import jax.numpy as jnp
from jax import lax
from jax.experimental import pallas as pl
from jax.experimental.pallas import tpu as pltpu
from jax.sharding import PartitionSpec as P

MESH = pl.DeviceIdType.MESH
F32, BF16 = jnp.float32, jnp.bfloat16
HD = 128
RUN = 256
PIECE = 64
WIDE = 1024
SHARD = 1024
SPAN = 1024
LOG2E = math.log2(math.e)
SCALE = LOG2E / math.sqrt(HD)
NEG = -1e30

KV, DEC, GAIN, GAINS, SQ, TOT, SO, ZS, XS = range(9)
LK, LV, LQ, ST, IN, LO = ((9 + 2 * i, 10 + 2 * i) for i in range(6))
KINDS = 21
HALF = WIDE // 2
SLICE = 32

NT = (((1,), (1,)), ((), ()))
TN = (((0,), (0,)), ((), ()))


def kernel(
    docs_ref, lq_ref, lk_ref, lv_ref, dec_ref, gain_ref, sq_ref, kv_ref,
    lo_ref, so_ref,
    lq, lk, lv, dec_out, dec, gains, inner, lout, part, tot, parts, tots, back, incoming,
    sq, kv, sout, cums, gain_out, send, recv, z_recv, left_recv, right_recv, far_recv,
):
    s = lax.axis_index("seq")
    h = lax.axis_index("head")
    y, c = s // 2, s % 2
    x, z = h // 4, h % 4
    group = c * 4 + z
    member = y * 4 + x

    def yc(d):
        return (s + d) % 8

    def zc(d):
        other = (group + d) % 8
        return other, (y * 2 + other // 4, x * 4 + other % 4)

    def along_x(d):
        return (s, ((x + d) % 4) * 4 + z)

    def along_z(d):
        return (s, x * 4 + (z + d) % 4)

    def xy(d):
        other = (member + d) % 16
        return other, ((other // 4) * 2 + c, (other % 4) * 4 + z)

    def push(kind, src, dst, device, recv_sem=None):
        pltpu.make_async_remote_copy(
            src_ref=src, dst_ref=dst, send_sem=send.at[kind],
            recv_sem=recv.at[kind] if recv_sem is None else recv_sem,
            device_id=device, device_id_type=MESH,
        ).start()

    def keep(kind, src, dst):
        pltpu.make_async_copy(src, dst, recv.at[kind]).start()

    def landed(sem, ref):
        pltpu.make_async_copy(ref, ref, sem).wait()

    def each(n, body):
        def step(d, carry):
            body(d)
            return carry
        lax.fori_loop(1, n, step, 0)

    barrier = pltpu.get_barrier_semaphore()

    def greet(device):
        pl.semaphore_signal(barrier, inc=1, device_id=device, device_id_type=MESH)

    each(8, lambda d: greet((yc(d), h)))
    each(8, lambda d: greet(zc(d)[1]))
    each(16, lambda d: greet(xy(d)[1]))
    gain = gain_ref[...].astype(F32)
    gain_out[...] = jnp.concatenate([gain, gain], axis=0)
    wide = jnp.concatenate([dec_ref[...], dec_ref[...]], axis=1).astype(F32)
    for g in range(8):
        dec_out[g] = (wide if g == 0 else pltpu.roll(wide, 128 - 8 * g, 1)).astype(BF16)
    pl.semaphore_wait(barrier, 7 + 7 + 15)

    mine = pl.ds(s * SHARD + h * PIECE, PIECE)

    def send_kv(d):
        to = yc(d)
        push(KV, kv_ref.at[:, pl.ds(to * HD, HD)], kv.at[mine, pl.ds(0, HD)], (to, h))
        push(KV, kv_ref.at[:, pl.ds(WIDE + to * HD, HD)], kv.at[mine, pl.ds(HD, HD)], (to, h))

    each(8, send_kv)
    keep(KV, kv_ref.at[:, pl.ds(s * HD, HD)], kv.at[mine, pl.ds(0, HD)])
    keep(KV, kv_ref.at[:, pl.ds(WIDE + s * HD, HD)], kv.at[mine, pl.ds(HD, HD)])

    rows = pl.ds(z * PIECE, PIECE)

    def send_light(kinds, half, ref, buf):
        place = buf.at[c, rows, pl.ds(half * HALF, HALF)]
        def one(d):
            other, device = zc(d)
            push(kinds[half], ref.at[:, pl.ds(other * WIDE + half * HALF, HALF)], place, device)
        each(8, one)
        keep(kinds[half], ref.at[:, pl.ds(group * WIDE + half * HALF, HALF)], place)

    def send_dec(d):
        other, device = zc(d)
        push(DEC, dec_out.at[other], dec.at[c, rows, :], device)

    each(8, send_dec)
    keep(DEC, dec_out.at[group], dec.at[c, rows, :])
    each(4, lambda d: push(GAIN, gain_out, gains.at[x, z], along_z(d)))
    keep(GAIN, gain_out, gains.at[x, z])
    send_light(LK, 0, lk_ref, lk)

    def send_sq(d):
        to = yc(d)
        push(SQ, sq_ref.at[:, pl.ds(to * WIDE, WIDE)], sq.at[s], (to, h))

    each(8, send_sq)
    keep(SQ, sq_ref.at[:, pl.ds(s * WIDE, WIDE)], sq.at[s])

    landed(recv.at[KV], kv.at[pl.ds(0, 8 * PIECE)])

    def send_z(t, carry):
        block_rows = kv.at[pl.ds(t * SHARD + h * PIECE, PIECE)]
        each(4, lambda d: push(ZS, block_rows, block_rows, along_z(d), z_recv.at[t]))
        return carry

    lax.fori_loop(0, 3, send_z, 0)
    send_light(LV, 0, lv_ref, lv)
    lax.fori_loop(3, 5, send_z, 0)
    send_light(LK, 1, lk_ref, lk)
    lax.fori_loop(5, 7, send_z, 0)
    send_light(LV, 1, lv_ref, lv)
    lax.fori_loop(7, 8, send_z, 0)
    send_light(LQ, 0, lq_ref, lq)
    send_light(LQ, 1, lq_ref, lq)
    landed(recv.at[GAIN], gains.at[0])
    each(4, lambda d: push(GAINS, gains.at[x], gains.at[x], along_x(d)))

    def send_near(t):
        landed(z_recv.at[t], kv.at[pl.ds(0, 3 * PIECE)])
        block_rows = kv.at[pl.ds(t * SHARD + x * RUN, RUN)]
        push(XS, block_rows, block_rows, along_x(1), left_recv.at[t])
        push(XS, block_rows, block_rows, along_x(3), right_recv.at[t])

    def pass_on(t):
        landed(left_recv.at[t], kv.at[pl.ds(0, RUN)])
        landed(right_recv.at[t], kv.at[pl.ds(0, RUN)])
        way = 1 + 2 * (t % 2)
        block_rows = kv.at[pl.ds(t * SHARD + ((x + 4 - way) % 4) * RUN, RUN)]
        push(XS, block_rows, block_rows, along_x(way), far_recv.at[t])

    ends = []
    total = jnp.int32(0)
    for i in range(8):
        total = total + docs_ref[i] * 128
        ends.append(total)

    def doc_of(pos):
        found = jnp.zeros_like(pos)
        for end in ends:
            found = found + jnp.where(pos >= end, 1, 0)
        return found

    column = lax.broadcasted_iota(jnp.int32, (RUN, 1), 0)
    line = lax.broadcasted_iota(jnp.int32, (1, RUN), 1)
    causal = column >= line
    lower = jnp.where(causal, 1.0, 0.0).astype(BF16)

    def run_start(i):
        return (2 * y + i) * SHARD + x * RUN

    def sum_decays(i, carry):
        cum = jnp.dot(lower, dec[i], preferred_element_type=F32)
        cums[i] = cum
        tot[i] = jnp.broadcast_to(cum.T[0:8, RUN - 1:RUN], (8, 128))
        return carry

    def states(half):
        if half == 0:
            landed(recv.at[DEC], dec)
            lax.fori_loop(0, 2, sum_decays, 0)
        landed(recv.at[LK[half]], lk.at[0])
        landed(recv.at[LV[half]], lv.at[0])

        def add_states(i, carry):
            cum = cums[i]
            start = run_start(i)
            last = doc_of(start + RUN - 1)
            tail = jnp.exp(cum[RUN - 1:RUN, :] - cum)
            tail = tail * jnp.where(doc_of(start + column) == last, 1.0, 0.0)
            for j in range(4 * half, 4 * half + 4):
                cols = pl.ds(j * HD, HD)
                weighted = (lv[i, :, cols].astype(F32) * tail[:, j:j + 1]).astype(BF16)
                added = lax.dot_general(lk[i, :, cols], weighted, TN, preferred_element_type=F32)
                part[i, cols, :] = added.astype(BF16)
            return carry

        lax.fori_loop(0, 2, add_states, 0)

        def send_state(d):
            other, device = xy(d)
            if half == 0:
                push(TOT, tot, tots.at[y, :, x], device)
            mine = part.at[:, pl.ds(half * HALF + other * SLICE, SLICE), :]
            push(ST[half], mine, parts.at[half, y, :, x], device)

        each(16, send_state)
        if half == 0:
            keep(TOT, tot, tots.at[y, :, x])
        mine = part.at[:, pl.ds(half * HALF + member * SLICE, SLICE), :]
        keep(ST[half], mine, parts.at[half, y, :, x])

    def within(half):
        landed(recv.at[LQ[half]], lq.at[0])

        def inner_run(i, carry):
            cum = cums[i]
            across = cum.T
            start = run_start(i)
            allowed = causal & (doc_of(start + column) == doc_of(start + line))
            for j in range(4 * half, 4 * half + 4):
                cols = pl.ds(j * HD, HD)
                gap = cum[:, j:j + 1] - across[j:j + 1, :]
                weight = jnp.exp(jnp.where(allowed, gap, NEG))
                scores = lax.dot_general(
                    lq[i, :, cols], lk[i, :, cols], NT, preferred_element_type=F32
                )
                inner[i, :, cols] = jnp.dot(
                    (scores * weight).astype(BF16), lv[i, :, cols], preferred_element_type=F32
                )
            return carry

        lax.fori_loop(0, 2, inner_run, 0)

    def entering_states(half):
        if half == 0:
            landed(recv.at[TOT], tots)
        landed(recv.at[ST[half]], parts.at[half])

        def scan_runs(p, state):
            a, b, e = p // 8, (p // 4) % 2, p % 4
            back[half, a, b, e] = state.astype(BF16)
            start = p * RUN
            same = jnp.where(doc_of(start + RUN - 1) == doc_of(start - 1), 1.0, 0.0)
            factor = jnp.exp(tots[a, b, e, pl.ds(half * 4 + member // 4, 1), :]) * same
            return state * factor + parts[half, a, b, e].astype(F32)

        lax.fori_loop(0, 32, scan_runs, jnp.zeros((SLICE, HD), F32))
        place = incoming.at[:, pl.ds(half * HALF + member * SLICE, SLICE), :]

        def send_back(d):
            other, device = xy(d)
            push(IN[half], back.at[half, other // 4, :, other % 4], place, device)

        each(16, send_back)
        keep(IN[half], back.at[half, y, :, x], place)

    token = lax.broadcasted_iota(jnp.int32, (8 * PIECE, 1), 0) % PIECE
    key_line = lax.broadcasted_iota(jnp.int32, (1, SPAN), 1)

    def soft_piece(t):
        first = t * SHARD + h * PIECE
        doc_start = jnp.int32(0)
        for end in ends:
            doc_start = jnp.where(first >= end, end, doc_start)
        query = jnp.concatenate([sq[t, :, pl.ds(j * HD, HD)] for j in range(8)], axis=0)

        def block(k, stats, diagonal):
            top, denominator, acc = stats
            limit = first + PIECE - SPAN * k
            start = pl.multiple_of(jnp.maximum(limit - SPAN, 0), PIECE)
            key_pos = start + key_line
            scores = lax.dot_general(
                query, kv[pl.ds(start, SPAN), pl.ds(0, HD)], NT, preferred_element_type=F32
            )
            if diagonal:
                kept = (key_pos >= doc_start) & (key_pos <= first + token)
                scores = jnp.where(kept, scores, NEG)
            else:
                kept = (key_pos >= doc_start) & (key_pos < limit)
                scores = scores + jnp.where(kept, 0.0, NEG)
            new_top = jnp.maximum(top, jnp.max(scores, axis=1, keepdims=True))
            weights = jnp.exp2((scores - new_top) * SCALE)
            summed = jnp.sum(weights, axis=1, keepdims=True)
            product = jnp.dot(
                weights.astype(BF16), kv[pl.ds(start, SPAN), pl.ds(HD, HD)],
                preferred_element_type=F32,
            )
            rescale = jnp.exp2((top - new_top) * SCALE)
            return new_top, denominator * rescale + summed, acc * rescale + product

        stats = (
            jnp.full((8 * PIECE, 1), NEG, F32),
            jnp.zeros((8 * PIECE, 1), F32),
            jnp.zeros((8 * PIECE, HD), F32),
        )
        older = jnp.minimum(t, 3)
        stats = lax.fori_loop(0, older, lambda k, st: block(older - k, st, False), stats)
        landed(far_recv.at[t], kv.at[pl.ds(0, RUN)])
        top, denominator, acc = block(0, stats, True)
        result = (acc / denominator).astype(BF16)
        for j in range(8):
            sout[t, :, pl.ds(j * HD, HD)] = result[j * PIECE:(j + 1) * PIECE, :]

        target = so_ref.at[:, pl.ds(s * WIDE, WIDE)]

        @pl.when(t == s)
        def _():
            keep(SO, sout.at[t], target)

        @pl.when(t != s)
        def _():
            push(SO, sout.at[t], target, (t, h))

    def light_outputs(half):
        if half == 0:
            landed(recv.at[GAINS], gains.at[pl.ds(0, 3)])
        landed(recv.at[IN[half]], incoming.at[0])

        def finish(i, carry):
            start = run_start(i)
            carried = jnp.where(doc_of(start + column) == doc_of(start - 1), 1.0, 0.0)
            reach = jnp.exp(cums[i]) * carried
            for j in range(4 * half, 4 * half + 4):
                cols = pl.ds(j * HD, HD)
                entering = jnp.dot(
                    lq[i, :, cols], incoming[i, cols, :], preferred_element_type=F32
                )
                mixed = inner[i, :, cols] + entering * reach[:, j:j + 1]
                mean_square = jnp.mean(mixed * mixed, axis=1, keepdims=True)
                source = 2 * group + half
                gain = gains[source // 4, source % 4, pl.ds(j % 4, 1), :]
                lout[i, :, cols] = (mixed * lax.rsqrt(mean_square + 1e-6) * gain).astype(BF16)
            return carry

        lax.fori_loop(0, 2, finish, 0)
        cols = pl.ds(half * HALF, HALF)
        target = lo_ref.at[:, pl.ds(group * WIDE + half * HALF, HALF)]

        def send_out(d):
            other, device = zc(d)
            source = lout.at[other // 4, pl.ds((other % 4) * PIECE, PIECE), cols]
            push(LO[half], source, target, device)

        each(8, send_out)
        keep(LO[half], lout.at[c, rows, cols], target)

    def step(t, carry):
        def at(n, work, *args):
            pl.when(t == n)(lambda: work(*args))

        pl.when((t >= 2) & (t < 10))(lambda: pass_on(t - 2))
        at(2, states, 0)
        at(6, states, 1)
        pl.when(t < 8)(lambda: send_near(t))
        at(5, entering_states, 0)
        at(8, entering_states, 1)
        at(8, within, 0)
        at(8, light_outputs, 0)
        at(9, within, 1)
        at(10, light_outputs, 1)
        at(3, lambda: landed(recv.at[SQ], sq))
        pl.when(t >= 3)(lambda: soft_piece(t - 3))
        return carry

    lax.fori_loop(0, 11, step, 0)

    landed(send.at[KV], kv.at[pl.ds(0, 7 * PIECE)])
    landed(send.at[DEC], dec_out.at[pl.ds(0, 7)])
    landed(send.at[GAIN], gains.at[0, pl.ds(0, 3)])
    landed(send.at[GAINS], gains.at[pl.ds(0, 3)])
    for kind in LK + LV + LQ + LO:
        landed(send.at[kind], lk.at[0, pl.ds(0, 7 * 32), :])
    for kind in (SQ, SO):
        landed(send.at[kind], sq.at[pl.ds(0, 7)])
    landed(send.at[ZS], kv.at[pl.ds(0, 24 * PIECE)])
    landed(send.at[XS], kv.at[pl.ds(0, 24 * RUN)])
    landed(send.at[TOT], inner.at[0, pl.ds(0, 15 * 16), pl.ds(0, HD)])
    for kind in ST + IN:
        landed(send.at[kind], kv.at[pl.ds(0, 15 * SLICE)])
    for kind in LO:
        landed(recv.at[kind], lo_ref.at[:, pl.ds(0, 4 * WIDE)])
    landed(recv.at[SO], so_ref)


def per_device(
    light_query, light_key, light_value, light_decay, light_gain, soft_query, soft_kv, doc_blocks
):
    gain = light_gain.reshape(4, HD)
    kv = soft_kv.reshape(PIECE, 2 * WIDE)
    anywhere = pl.BlockSpec(memory_space=pl.ANY)
    vmem = pl.BlockSpec(memory_space=pltpu.VMEM)
    out = jax.ShapeDtypeStruct((PIECE, 8 * WIDE), BF16)
    scratch = [
        pltpu.VMEM((2, RUN, WIDE), BF16),
        pltpu.VMEM((2, RUN, WIDE), BF16),
        pltpu.VMEM((2, RUN, WIDE), BF16),
        pltpu.VMEM((8, PIECE, 128), BF16),
        pltpu.VMEM((2, RUN, 128), BF16),
        pltpu.VMEM((4, 4, 8, HD), F32),
        pltpu.VMEM((2, RUN, WIDE), F32),
        pltpu.VMEM((2, RUN, WIDE), BF16),
        pltpu.VMEM((2, WIDE, HD), BF16),
        pltpu.VMEM((2, 8, 128), F32),
        pltpu.VMEM((2, 4, 2, 4, SLICE, HD), BF16),
        pltpu.VMEM((4, 2, 4, 8, 128), F32),
        pltpu.VMEM((2, 4, 2, 4, SLICE, HD), BF16),
        pltpu.VMEM((2, WIDE, HD), BF16),
        pltpu.VMEM((8, PIECE, WIDE), BF16),
        pltpu.VMEM((8 * SHARD, 2 * HD), BF16),
        pltpu.VMEM((8, PIECE, WIDE), BF16),
        pltpu.VMEM((2, RUN, 128), F32),
        pltpu.VMEM((8, HD), F32),
        pltpu.SemaphoreType.DMA((KINDS,)),
        pltpu.SemaphoreType.DMA((KINDS,)),
        pltpu.SemaphoreType.DMA((8,)),
        pltpu.SemaphoreType.DMA((8,)),
        pltpu.SemaphoreType.DMA((8,)),
        pltpu.SemaphoreType.DMA((8,)),
    ]
    return pl.pallas_call(
        kernel,
        out_shape=(out, out),
        in_specs=[
            pl.BlockSpec(memory_space=pltpu.SMEM), anywhere, anywhere, anywhere, vmem, vmem,
            anywhere, anywhere,
        ],
        out_specs=(anywhere, anywhere),
        scratch_shapes=scratch,
        compiler_params=pltpu.CompilerParams(
            collective_id=0, has_side_effects=True, vmem_limit_bytes=63 * 2**20
        ),
    )(doc_blocks, light_query, light_key, light_value, light_decay, gain, soft_query, kv)


def solution(mesh):
    placed = (
        P(("seq", "head"), None),
        P(("seq", "head"), None),
        P(("seq", "head"), None),
        P(("seq", "head"), None),
        P("head"),
        P(("seq", "head"), None),
        P(("seq", "head"), None, None),
        P(),
    )
    return jax.shard_map(
        per_device,
        mesh=mesh,
        in_specs=placed,
        out_specs=(P(("seq", "head"), None), P(("seq", "head"), None)),
        check_vma=False,
    )
```

time: 144 us -> 96.6 us (0.67)
  Pallas kernels: 135 us -> 90.7 us
  local copies, waits for them, and re-layouts: 7.94 us -> 5.03 us
    pallas_call x1, Pallas kernels: 135 us -> 90.7 us  [per_device(): pl.pallas_call(kernel, out_shape=(out, out), in_specs=[pl.BlockSpec(memor...]
    unnamed x15 -> x5, local copies, waits for them, and re-layouts: 7.94 us -> 5.03 us
where the time goes in v2:
time: 96.6 us; the launch traced here: 96.4 us
  Pallas kernels  90.7 us (94%)
  local copies, waits for them, and re-layouts  5.03 us (5%)
    pallas_call x1, Pallas kernels, per_device(): pl.pallas_call(kernel, out_shape=(out, out), in_specs=[pl.BlockSpec(memor...  90.7 us
    unnamed x5, local copies, waits for them, and re-layouts  5.03 us

profile of v2, /device:TPU:25, one launch (start us, length us, event | category | flops | bytes accessed | tf_op | source)
XLA Modules:
  0.0 96.4 jit_solution(17976491023556385050)
XLA Ops:
  0.6 1.7 %copy.10 = bf16[8,8,2,1024]{3,1,2,0:T(8,128)(2,1)} copy(bf16[8,8,2,1024]{3,2,1,0:T(2,128)(2,1)} %bitcast.4) | data formatting | bytes 524288
  2.3 90.7 %shard_map.95 = (bf16[64,8192]{1,0:T(8,128)(2,1)}, bf16[64,8192]{1,0:T(8,128)(2,1)}) custom-call(s32[8]{0:T(128)} %docs_ref.1, bf16[64,8192]{1,0:T(8,128)(2,1)} %lq_ref.1, bf16[64,8192]{1,0:T(8,128)(2,1)} %lk_ref.1, bf16[64,8192]{1,0:T(8,128)(2,1)} %lv_ref.1, bf16[64,64]{1,0:T(8,128)(2,1)} %dec_ref.1, bf16[4,128]{1,0:T(4,128)(2,1)} %bitcast.5, ...), custom_call_target="tpu_custom_call" | custom-call | tf_op jit(solution)/shard_map/pallas_call | solution.py:436
  93.1 0.0 copy-start
  93.1 2.4 %copy.13 = bf16[64,8192]{1,0:T(8,128)(2,1)} copy(bf16[64,8192]{1,0:T(8,128)(2,1)} %get-tuple-element.4) | data formatting | bytes 2097152
  95.5 0.0 copy-done
  95.5 1.0 %copy.14 = bf16[64,8192]{1,0:T(8,128)(2,1)} copy(bf16[64,8192]{1,0:T(8,128)(2,1)S(1)} %copy-done) | data formatting | bytes 2097152
Async XLA Ops:
  93.1 2.4 %copy-start = (bf16[64,8192]{1,0:T(8,128)(2,1)S(1)}, bf16[64,8192]{1,0:T(8,128)(2,1)}, u32[]{:S(2)}) copy-start(bf16[64,8192]{1,0:T(8,128)(2,1)} %get-tuple-element.5) | copy-start | bytes 3145732

commit v3 on v2

v3 whole, which is shorter than its diff:
```python
import functools
import itertools
import math

import jax
import jax.numpy as jnp
from jax import lax
from jax.experimental import pallas as pl
from jax.experimental.pallas import tpu as pltpu
from jax.sharding import PartitionSpec as P

MESH = pl.DeviceIdType.MESH
F32, BF16 = jnp.float32, jnp.bfloat16
HD = 128
RUN = 256
PIECE = 64
WIDE = 1024
SHARD = 1024
SPAN = 1024
ROWS = 8 * PIECE
LOG2E = math.log2(math.e)
SCALE = LOG2E / math.sqrt(HD)
NEG = -1e30

KV, DEC, GAIN, GAINS, SQ, TOT, SO, ZS, XS = range(9)
LK, LV, LQ, ST, IN, LO = ((9 + 2 * i, 10 + 2 * i) for i in range(6))
KINDS = 21
SPLIT = ((0, 6), (6, 2))
SLICE = (48, 16)

NT = (((1,), (1,)), ((), ()))
TN = (((0,), (0,)), ((), ()))


def kernel(
    docs_ref, lq_ref, lk_ref, lv_ref, dec_ref, gain_ref, sq_ref, kv_ref,
    lo_ref, so_ref,
    lq, lk, lv, dec_out, dec, gains, inner, lout, part, tot, parts0, parts1, tots, back0, back1, incoming, factors,
    sq, kv, kv_out, sout, cums, gain_out, queries, marks, top, denominator, acc, send, recv, z_recv, left_recv, right_recv, far_recv,
):
    s = lax.axis_index("seq")
    h = lax.axis_index("head")
    y, c = s // 2, s % 2
    x, z = h // 4, h % 4
    group = c * 4 + z
    member = y * 4 + x

    parts, back = (parts0, parts1), (back0, back1)

    def part_cols(half, start=0):
        first, heads = SPLIT[half]
        return pl.ds(start + first * HD, heads * HD)

    def part_heads(half):
        first, heads = SPLIT[half]
        return range(first, first + heads)

    def yc(d):
        return (s + d) % 8

    def zc(d):
        other = (group + d) % 8
        return other, (y * 2 + other // 4, x * 4 + other % 4)

    def along_x(d):
        return (s, ((x + d) % 4) * 4 + z)

    def along_z(d):
        return (s, x * 4 + (z + d) % 4)

    def xy(d):
        other = (member + d) % 16
        return other, ((other // 4) * 2 + c, (other % 4) * 4 + z)

    def push(kind, src, dst, device, recv_sem=None):
        pltpu.make_async_remote_copy(
            src_ref=src, dst_ref=dst, send_sem=send.at[kind],
            recv_sem=recv.at[kind] if recv_sem is None else recv_sem,
            device_id=device, device_id_type=MESH,
        ).start()

    def keep(kind, src, dst):
        pltpu.make_async_copy(src, dst, recv.at[kind]).start()

    def landed(sem, ref):
        pltpu.make_async_copy(ref, ref, sem).wait()

    def each(n, body):
        def step(d, carry):
            body(d)
            return carry
        lax.fori_loop(1, n, step, 0)

    barrier = pltpu.get_barrier_semaphore()

    def greet(device):
        pl.semaphore_signal(barrier, inc=1, device_id=device, device_id_type=MESH)

    each(8, lambda d: greet((yc(d), h)))
    each(8, lambda d: greet(zc(d)[1]))
    each(16, lambda d: greet(xy(d)[1]))
    gain = gain_ref[...].astype(F32)
    gain_out[...] = jnp.concatenate([gain, gain], axis=0)
    wide = jnp.concatenate([dec_ref[...], dec_ref[...]], axis=1).astype(F32)
    for g in range(8):
        dec_out[g] = (wide if g == 0 else pltpu.roll(wide, 128 - 8 * g, 1)).astype(BF16)
    for g in range(8):
        for i in range(2):
            kv_out[g, :, pl.ds(i * HD, HD)] = kv_ref[:, i, pl.ds(g * HD, HD)]
    pl.semaphore_wait(barrier, 7 + 7 + 15)

    mine = pl.ds(SHARD + s * SHARD + h * PIECE, PIECE)

    def send_kv(d):
        to = yc(d)
        push(KV, kv_out.at[to], kv.at[mine], (to, h))

    each(8, send_kv)
    keep(KV, kv_out.at[s], kv.at[mine])

    rows = pl.ds(z * PIECE, PIECE)

    def send_light(kinds, half, ref, buf, some=None):
        first, heads = some or SPLIT[half]
        place = buf.at[c, rows, pl.ds(first * HD, heads * HD)]
        def one(d):
            other, device = zc(d)
            source = ref.at[:, pl.ds(other * WIDE + first * HD, heads * HD)]
            push(kinds[half], source, place, device)
        each(8, one)
        keep(kinds[half], ref.at[:, pl.ds(group * WIDE + first * HD, heads * HD)], place)

    def send_dec(d):
        other, device = zc(d)
        push(DEC, dec_out.at[other], dec.at[c, rows, :], device)

    each(8, send_dec)
    keep(DEC, dec_out.at[group], dec.at[c, rows, :])
    each(4, lambda d: push(GAIN, gain_out, gains.at[x, z], along_z(d)))
    keep(GAIN, gain_out, gains.at[x, z])
    send_light(LK, 0, lk_ref, lk, (0, 4))

    ends = []
    total = jnp.int32(0)
    for i in range(8):
        total = total + docs_ref[i] * 128
        ends.append(total)

    def doc_of(pos):
        found = jnp.zeros_like(pos)
        for end in ends:
            found = found + jnp.where(pos >= end, 1, 0)
        return found

    lane = lax.broadcasted_iota(jnp.int32, (1, HD), 1)
    doc_first = jnp.zeros((1, HD), jnp.int32)
    doc_end = jnp.zeros((1, HD), jnp.int32)
    for i, end in enumerate(ends):
        doc_first = jnp.where(lane == i, ends[i - 1] if i else 0, doc_first)
        doc_end = jnp.where(lane == i, end, doc_end)

    def mark(n, carry):
        at_row = pl.ds(pl.multiple_of(n * SHARD, SHARD), SHARD)
        row = lax.broadcasted_iota(jnp.int32, (SHARD, HD), 0)
        lanes = lax.broadcasted_iota(jnp.int32, (SHARD, HD), 1)
        token = (n - 1) * SHARD + row
        in_doc = (token >= doc_first) & (token < doc_end)
        own = (row == h * PIECE + lanes - 64) & (lanes >= 64)
        outside = (lanes == 8) & (token < 0)
        marks[at_row, :] = jnp.where(in_doc | own | outside, 1.0, 0.0).astype(BF16)
        return carry

    lax.fori_loop(0, 9, mark, 0)
    kv[pl.ds(0, SHARD), :] = jnp.zeros((SHARD, 2 * HD), BF16)

    landed(recv.at[KV], kv.at[pl.ds(0, 8 * PIECE)])

    def send_z(t, carry):
        block_rows = kv.at[pl.ds(SHARD + t * SHARD + h * PIECE, PIECE)]
        each(4, lambda d: push(ZS, block_rows, block_rows, along_z(d), z_recv.at[t]))
        return carry

    lax.fori_loop(0, 4, send_z, 0)
    def send_sq(d):
        to = yc(d)
        push(SQ, sq_ref.at[:, pl.ds(to * WIDE, WIDE)], sq.at[s], (to, h))

    each(8, send_sq)
    keep(SQ, sq_ref.at[:, pl.ds(s * WIDE, WIDE)], sq.at[s])

    send_light(LK, 0, lk_ref, lk, (4, 2))
    send_light(LV, 0, lv_ref, lv)
    lax.fori_loop(4, 6, send_z, 0)
    send_light(LK, 1, lk_ref, lk)
    send_light(LV, 1, lv_ref, lv)
    lax.fori_loop(6, 8, send_z, 0)
    send_light(LQ, 0, lq_ref, lq)
    send_light(LQ, 1, lq_ref, lq)
    landed(recv.at[GAIN], gains.at[0])
    each(4, lambda d: push(GAINS, gains.at[x], gains.at[x], along_x(d)))

    def continues(p, carry):
        same = jnp.where(doc_of(p * RUN + RUN - 1) == doc_of(p * RUN - 1), 1.0, 0.0)
        factors[p // 8, (p // 4) % 2, p % 4] = jnp.full((8, 128), same, F32)
        return carry

    def prepare():
        lax.fori_loop(0, 32, continues, 0)
        top[...] = jnp.full_like(top, NEG)
        denominator[...] = jnp.zeros_like(denominator)
        acc[...] = jnp.zeros_like(acc)

    def send_near(t):
        landed(z_recv.at[t], kv.at[pl.ds(0, 3 * PIECE)])
        block_rows = kv.at[pl.ds(SHARD + t * SHARD + x * RUN, RUN)]
        push(XS, block_rows, block_rows, along_x(1), left_recv.at[t])
        push(XS, block_rows, block_rows, along_x(3), right_recv.at[t])

    def pass_on(t):
        landed(left_recv.at[t], kv.at[pl.ds(0, RUN)])
        landed(right_recv.at[t], kv.at[pl.ds(0, RUN)])
        way = 1 + 2 * (t % 2)
        block_rows = kv.at[pl.ds(SHARD + t * SHARD + ((x + 4 - way) % 4) * RUN, RUN)]
        push(XS, block_rows, block_rows, along_x(way), far_recv.at[t])

    column = lax.broadcasted_iota(jnp.int32, (RUN, 1), 0)
    line = lax.broadcasted_iota(jnp.int32, (1, RUN), 1)
    causal = column >= line
    lower = jnp.where(causal, 1.0, 0.0).astype(BF16)

    def run_start(i):
        return (2 * y + i) * SHARD + x * RUN

    def sum_decays(i, carry):
        cum = jnp.dot(lower, dec[i], preferred_element_type=F32)
        cums[i] = cum
        tot[i] = jnp.broadcast_to(cum.T[0:8, RUN - 1:RUN], (8, 128))
        return carry

    def slice_rows(half, owner):
        return pl.ds(SPLIT[half][0] * HD + owner * SLICE[half], SLICE[half])

    def states(half):
        if half == 0:
            landed(recv.at[DEC], dec)
            lax.fori_loop(0, 2, sum_decays, 0)
        landed(recv.at[LK[half]], lk.at[:, :, part_cols(half)])
        landed(recv.at[LV[half]], lv.at[:, :, part_cols(half)])

        def add_states(i, carry):
            cum = cums[i]
            start = run_start(i)
            last = doc_of(start + RUN - 1)
            tail = jnp.exp(cum[RUN - 1:RUN, :] - cum)
            tail = tail * jnp.where(doc_of(start + column) == last, 1.0, 0.0)
            for j in part_heads(half):
                cols = pl.ds(j * HD, HD)
                weighted = (lv[i, :, cols].astype(F32) * tail[:, j:j + 1]).astype(BF16)
                added = lax.dot_general(lk[i, :, cols], weighted, TN, preferred_element_type=F32)
                part[i, cols, :] = added.astype(BF16)
            return carry

        lax.fori_loop(0, 2, add_states, 0)

        def send_state(d):
            other, device = xy(d)
            if half == 0:
                push(TOT, tot, tots.at[y, :, x], device)
            mine = part.at[:, slice_rows(half, other), :]
            push(ST[half], mine, parts[half].at[y, :, x], device)

        each(16, send_state)
        if half == 0:
            keep(TOT, tot, tots.at[y, :, x])
        mine = part.at[:, slice_rows(half, member), :]
        keep(ST[half], mine, parts[half].at[y, :, x])

    def within(half):
        landed(recv.at[LQ[half]], lq.at[:, :, part_cols(half)])

        def inner_run(i, carry):
            cum = cums[i]
            across = cum.T
            start = run_start(i)
            allowed = causal & (doc_of(start + column) == doc_of(start + line))
            for j in part_heads(half):
                cols = pl.ds(j * HD, HD)
                gap = cum[:, j:j + 1] - across[j:j + 1, :]
                weight = jnp.exp(jnp.where(allowed, gap, NEG))
                scores = lax.dot_general(
                    lq[i, :, cols], lk[i, :, cols], NT, preferred_element_type=F32
                )
                inner[i, :, cols] = jnp.dot(
                    (scores * weight).astype(BF16), lv[i, :, cols], preferred_element_type=F32
                )
            return carry

        lax.fori_loop(0, 2, inner_run, 0)

    def entering_states(half):
        if half == 0:
            landed(recv.at[TOT], tots)
            factors[...] = factors[...] * jnp.exp(tots[...])
        landed(recv.at[ST[half]], parts[half])
        own_first = member * SLICE[half]
        head = own_first // HD
        after = jnp.minimum(head + 1, SPLIT[half][1] - 1)
        in_head = own_first + lax.broadcasted_iota(jnp.int32, (SLICE[half], HD), 0) < (head + 1) * HD

        state = jnp.zeros((SLICE[half], HD), F32)
        for a, b, e in itertools.product(range(4), range(2), range(4)):
            back[half][a, b, e] = state.astype(BF16)
            one = factors[a, b, e, pl.ds(SPLIT[half][0] + head, 1), :]
            two = factors[a, b, e, pl.ds(SPLIT[half][0] + after, 1), :]
            state = state * jnp.where(in_head, one, two) + parts[half][a, b, e].astype(F32)
        place = incoming.at[:, slice_rows(half, member), :]

        def send_back(d):
            other, device = xy(d)
            push(IN[half], back[half].at[other // 4, :, other % 4], place, device)

        each(16, send_back)
        keep(IN[half], back[half].at[y, :, x], place)

    def take_queries(t, carry):
        first = t * SHARD + h * PIECE
        inside = (first >= doc_first) & (first < doc_end)
        kept = jnp.where((lane > 8) | inside, 0.0, NEG).astype(BF16)
        for j in range(8):
            at_row = pl.ds(pl.multiple_of(t * ROWS, ROWS) + j * PIECE, PIECE)
            queries[at_row, pl.ds(0, HD)] = sq[t, :, pl.ds(j * HD, HD)]
            queries[at_row, pl.ds(HD, HD)] = jnp.broadcast_to(kept, (PIECE, HD))
        return carry

    def all_queries():
        landed(recv.at[SQ], sq)
        lax.fori_loop(0, 8, take_queries, 0)

    def key_block(t, count):
        first_row = pl.multiple_of(t * ROWS, ROWS)
        at_rows = pl.ds(first_row, count * ROWS)
        start = pl.multiple_of(t * SHARD + h * PIECE + PIECE, PIECE)
        keys = jnp.concatenate(
            [kv[pl.ds(start, SPAN), pl.ds(0, HD)], marks[pl.ds(start, SPAN), :]], axis=1
        )
        scores = lax.dot_general(queries[at_rows, :], keys, NT, preferred_element_type=F32)
        tiles = [scores[:, i * HD:(i + 1) * HD] for i in range(SPAN // HD)]
        highest = functools.reduce(jnp.maximum, tiles)
        old = top[at_rows, :]
        new = jnp.maximum(old, jnp.broadcast_to(jnp.max(highest, axis=1, keepdims=True), old.shape))
        top[at_rows, :] = new
        rescale = jnp.exp2((old - new) * SCALE)
        weights = [jnp.exp2((tile - new) * SCALE) for tile in tiles]
        denominator[at_rows, :] = functools.reduce(jnp.add, weights, denominator[at_rows, :] * rescale)
        rounded = jnp.concatenate([w.astype(BF16) for w in weights], axis=1)
        product = jnp.dot(rounded, kv[pl.ds(start, SPAN), pl.ds(HD, HD)], preferred_element_type=F32)
        acc[at_rows, :] = acc[at_rows, :] * rescale + product

    def soft_piece(t):
        landed(far_recv.at[t], kv.at[pl.ds(0, RUN)])
        at_rows = pl.ds(pl.multiple_of(t * ROWS, ROWS), ROWS)
        token = lax.broadcasted_iota(jnp.int32, (ROWS, HD), 0) % PIECE
        lanes = lax.broadcasted_iota(jnp.int32, (ROWS, HD), 1)
        kept = queries[at_rows, pl.ds(HD, HD)].astype(F32)
        queries[at_rows, pl.ds(HD, HD)] = jnp.where(lanes - 64 > token, NEG, kept).astype(BF16)
        pl.when(t <= 4)(lambda: key_block(t, 4))
        for last in (5, 6, 7):
            pl.when(t == last)(functools.partial(key_block, t, 8 - last))
        whole = jnp.sum(denominator[at_rows, :], axis=1, keepdims=True)
        result = (acc[at_rows, :] / whole).astype(BF16)
        for j in range(8):
            sout[t, :, pl.ds(j * HD, HD)] = result[j * PIECE:(j + 1) * PIECE, :]

        target = so_ref.at[:, pl.ds(s * WIDE, WIDE)]

        @pl.when(t == s)
        def _():
            keep(SO, sout.at[t], target)

        @pl.when(t != s)
        def _():
            push(SO, sout.at[t], target, (t, h))

    def light_outputs(half):
        if half == 0:
            landed(recv.at[GAINS], gains.at[pl.ds(0, 3)])
        landed(recv.at[IN[half]], incoming.at[:, part_cols(half), :])

        def finish(i, carry):
            start = run_start(i)
            carried = jnp.where(doc_of(start + column) == doc_of(start - 1), 1.0, 0.0)
            reach = jnp.exp(cums[i]) * carried
            for j in part_heads(half):
                cols = pl.ds(j * HD, HD)
                entering = jnp.dot(
                    lq[i, :, cols], incoming[i, cols, :], preferred_element_type=F32
                )
                mixed = inner[i, :, cols] + entering * reach[:, j:j + 1]
                mean_square = jnp.mean(mixed * mixed, axis=1, keepdims=True)
                source = 2 * group + j // 4
                gain = gains[source // 4, source % 4, pl.ds(j % 4, 1), :]
                lout[i, :, cols] = (mixed * lax.rsqrt(mean_square + 1e-6) * gain).astype(BF16)
            return carry

        lax.fori_loop(0, 2, finish, 0)
        cols = part_cols(half)
        target = lo_ref.at[:, part_cols(half, group * WIDE)]

        def send_out(d):
            other, device = zc(d)
            source = lout.at[other // 4, pl.ds((other % 4) * PIECE, PIECE), cols]
            push(LO[half], source, target, device)

        each(8, send_out)
        keep(LO[half], lout.at[c, rows, cols], target)

    def step(t, carry):
        def at(n, work, *args):
            pl.when(t == n)(lambda: work(*args))

        pl.when(t < 4)(lambda: send_near(t))
        pl.when((t >= 2) & (t < 5))(lambda: pass_on(t - 2))
        at(3, prepare)
        at(3, all_queries)
        pl.when(t >= 4)(lambda: soft_piece(t - 4))
        at(4, states, 0)
        at(4, send_near, 4)
        at(4, send_near, 5)
        at(4, pass_on, 3)
        at(6, states, 1)
        at(6, send_near, 6)
        at(7, entering_states, 0)
        at(7, send_near, 7)
        pl.when((t >= 6) & (t < 10))(lambda: pass_on(t - 2))
        at(8, entering_states, 1)
        at(8, within, 0)
        at(8, light_outputs, 0)
        at(9, within, 1)
        at(9, light_outputs, 1)
        return carry

    lax.fori_loop(0, 12, step, 0)

    landed(send.at[KV], kv.at[pl.ds(0, 7 * PIECE)])
    landed(send.at[DEC], dec_out.at[pl.ds(0, 7)])
    landed(send.at[GAIN], gains.at[0, pl.ds(0, 3)])
    landed(send.at[GAINS], gains.at[pl.ds(0, 3)])
    for kinds in (LK, LV, LQ, LO):
        for half in range(2):
            landed(send.at[kinds[half]], lk.at[:, pl.ds(0, 7 * 32), part_cols(half)])
    for kind in (SQ, SO):
        landed(send.at[kind], sq.at[pl.ds(0, 7)])
    landed(send.at[ZS], kv.at[pl.ds(0, 24 * PIECE)])
    landed(send.at[XS], kv.at[pl.ds(0, 24 * RUN)])
    landed(send.at[TOT], inner.at[0, pl.ds(0, 15 * 16), pl.ds(0, HD)])
    for half in range(2):
        for kind in (ST[half], IN[half]):
            landed(send.at[kind], kv.at[pl.ds(0, 15 * SLICE[half])])
        landed(recv.at[LO[half]], lo_ref.at[:, pl.ds(0, 8 * SPLIT[half][1] * HD)])
    landed(recv.at[SO], so_ref)


def per_device(
    light_query, light_key, light_value, light_decay, light_gain, soft_query, soft_kv, doc_blocks
):
    gain = light_gain.reshape(4, HD)
    anywhere = pl.BlockSpec(memory_space=pl.ANY)
    vmem = pl.BlockSpec(memory_space=pltpu.VMEM)
    out = jax.ShapeDtypeStruct((PIECE, 8 * WIDE), BF16)
    scratch = [
        pltpu.VMEM((2, RUN, WIDE), BF16),
        pltpu.VMEM((2, RUN, WIDE), BF16),
        pltpu.VMEM((2, RUN, WIDE), BF16),
        pltpu.VMEM((8, PIECE, 128), BF16),
        pltpu.VMEM((2, RUN, 128), BF16),
        pltpu.VMEM((4, 4, 8, HD), F32),
        pltpu.VMEM((2, RUN, WIDE), F32),
        pltpu.VMEM((2, RUN, WIDE), BF16),
        pltpu.VMEM((2, WIDE, HD), BF16),
        pltpu.VMEM((2, 8, 128), F32),
        pltpu.VMEM((4, 2, 4, SLICE[0], HD), BF16),
        pltpu.VMEM((4, 2, 4, SLICE[1], HD), BF16),
        pltpu.VMEM((4, 2, 4, 8, 128), F32),
        pltpu.VMEM((4, 2, 4, SLICE[0], HD), BF16),
        pltpu.VMEM((4, 2, 4, SLICE[1], HD), BF16),
        pltpu.VMEM((2, WIDE, HD), BF16),
        pltpu.VMEM((4, 2, 4, 8, 128), F32),
        pltpu.VMEM((8, PIECE, WIDE), BF16),
        pltpu.VMEM((9 * SHARD, 2 * HD), BF16),
        pltpu.VMEM((8, PIECE, 2 * HD), BF16),
        pltpu.VMEM((8, PIECE, WIDE), BF16),
        pltpu.VMEM((2, RUN, 128), F32),
        pltpu.VMEM((8, HD), F32),
        pltpu.VMEM((8 * ROWS, 2 * HD), BF16),
        pltpu.VMEM((9 * SHARD, HD), BF16),
        pltpu.VMEM((8 * ROWS, HD), F32),
        pltpu.VMEM((8 * ROWS, HD), F32),
        pltpu.VMEM((8 * ROWS, HD), F32),
        pltpu.SemaphoreType.DMA((KINDS,)),
        pltpu.SemaphoreType.DMA((KINDS,)),
        pltpu.SemaphoreType.DMA((8,)),
        pltpu.SemaphoreType.DMA((8,)),
        pltpu.SemaphoreType.DMA((8,)),
        pltpu.SemaphoreType.DMA((8,)),
    ]
    return pl.pallas_call(
        kernel,
        out_shape=(out, out),
        in_specs=[
            pl.BlockSpec(memory_space=pltpu.SMEM), anywhere, anywhere, anywhere, vmem, vmem,
            anywhere, vmem,
        ],
        out_specs=(anywhere, anywhere),
        scratch_shapes=scratch,
        compiler_params=pltpu.CompilerParams(
            collective_id=0, has_side_effects=True, vmem_limit_bytes=63 * 2**20
        ),
    )(doc_blocks, light_query, light_key, light_value, light_decay, gain, soft_query, soft_kv)


def solution(mesh):
    placed = (
        P(("seq", "head"), None),
        P(("seq", "head"), None),
        P(("seq", "head"), None),
        P(("seq", "head"), None),
        P("head"),
        P(("seq", "head"), None),
        P(("seq", "head"), None, None),
        P(),
    )
    return jax.shard_map(
        per_device,
        mesh=mesh,
        in_specs=placed,
        out_specs=(P(("seq", "head"), None), P(("seq", "head"), None)),
        check_vma=False,
    )
```

time: 96.6 us -> 88.1 us (0.912); the launches traced: 96.4 us -> 86.6 us
  Pallas kernels: 90.7 us -> 82.6 us
  local copies, waits for them, and re-layouts: 5.03 us -> 3.32 us
    pallas_call x1, Pallas kernels: 90.7 us -> 82.6 us  [per_device(): pl.pallas_call(kernel, out_shape=(out, out), in_specs=[pl.BlockSpec(memor...]
    unnamed x5 -> x4, local copies, waits for them, and re-layouts: 5.03 us -> 3.32 us
where the time goes in v3:
time: 88.1 us; the launch traced here: 86.6 us
  Pallas kernels  82.6 us (94%)
  local copies, waits for them, and re-layouts  3.32 us (4%)
    pallas_call x1, Pallas kernels, per_device(): pl.pallas_call(kernel, out_shape=(out, out), in_specs=[pl.BlockSpec(memor...  82.6 us
    unnamed x4, local copies, waits for them, and re-layouts  3.32 us

profile of v3, /device:TPU:25, one launch (start us, length us, event | category | flops | bytes accessed | tf_op | source)
XLA Modules:
  0.0 86.6 jit_solution(4722973376772410558)
XLA Ops:
  0.6 82.6 %shard_map.95 = (bf16[64,8192]{1,0:T(8,128)(2,1)}, bf16[64,8192]{1,0:T(8,128)(2,1)}) custom-call(s32[8]{0:T(128)} %docs_ref.1, bf16[64,8192]{1,0:T(8,128)(2,1)} %lq_ref.1, bf16[64,8192]{1,0:T(8,128)(2,1)} %lk_ref.1, bf16[64,8192]{1,0:T(8,128)(2,1)} %lv_ref.1, bf16[64,64]{1,0:T(8,128)(2,1)} %dec_ref.1, bf16[4,128]{1,0:T(4,128)(2,1)} %bitcast.1, ...), custom_call_target="tpu_custom_call" | custom-call | tf_op jit(solution)/shard_map/pallas_call | solution.py:506
  83.2 0.0 copy-start
  83.2 2.4 %copy.12 = bf16[64,8192]{1,0:T(8,128)(2,1)} copy(bf16[64,8192]{1,0:T(8,128)(2,1)} %get-tuple-element.4) | data formatting | bytes 2097152
  85.6 0.0 copy-done
  85.6 1.0 %copy.13 = bf16[64,8192]{1,0:T(8,128)(2,1)} copy(bf16[64,8192]{1,0:T(8,128)(2,1)S(1)} %copy-done) | data formatting | bytes 2097152
Async XLA Ops:
  83.2 2.4 %copy-start = (bf16[64,8192]{1,0:T(8,128)(2,1)S(1)}, bf16[64,8192]{1,0:T(8,128)(2,1)}, u32[]{:S(2)}) copy-start(bf16[64,8192]{1,0:T(8,128)(2,1)} %get-tuple-element.5) | copy-start | bytes 3145732

commit v4 on v3

--- a/solution.py
+++ b/solution.py
@@ -36,7 +36,7 @@
     docs_ref, lq_ref, lk_ref, lv_ref, dec_ref, gain_ref, sq_ref, kv_ref,
     lo_ref, so_ref,
     lq, lk, lv, dec_out, dec, gains, inner, lout, part, tot, parts0, parts1, tots, back0, back1, incoming, factors,
-    sq, kv, kv_out, sout, cums, gain_out, queries, marks, top, denominator, acc, send, recv, z_recv, left_recv, right_recv, far_recv,
+    sq, kv, kv_out, sout, cums, gain_out, queries, marks, top, denominator, acc, send, recv, kv_recv, z_recv, left_recv, right_recv, far_recv,
 ):
     s = lax.axis_index("seq")
     h = lax.axis_index("head")
@@ -113,10 +113,10 @@
 
     def send_kv(d):
         to = yc(d)
-        push(KV, kv_out.at[to], kv.at[mine], (to, h))
+        push(KV, kv_out.at[to], kv.at[mine], (to, h), kv_recv.at[s])
 
     each(8, send_kv)
-    keep(KV, kv_out.at[s], kv.at[mine])
+    pltpu.make_async_copy(kv_out.at[s], kv.at[mine], kv_recv.at[s]).start()
 
     rows = pl.ds(z * PIECE, PIECE)
 
@@ -134,11 +134,7 @@
         other, device = zc(d)
         push(DEC, dec_out.at[other], dec.at[c, rows, :], device)
 
-    each(8, send_dec)
-    keep(DEC, dec_out.at[group], dec.at[c, rows, :])
-    each(4, lambda d: push(GAIN, gain_out, gains.at[x, z], along_z(d)))
-    keep(GAIN, gain_out, gains.at[x, z])
-    send_light(LK, 0, lk_ref, lk, (0, 4))
+    send_light(LK, 0, lk_ref, lk, (0, 2))
 
     ends = []
     total = jnp.int32(0)
@@ -173,9 +169,9 @@
     lax.fori_loop(0, 9, mark, 0)
     kv[pl.ds(0, SHARD), :] = jnp.zeros((SHARD, 2 * HD), BF16)
 
-    landed(recv.at[KV], kv.at[pl.ds(0, 8 * PIECE)])
 
     def send_z(t, carry):
+        landed(kv_recv.at[t], kv.at[pl.ds(0, PIECE)])
         block_rows = kv.at[pl.ds(SHARD + t * SHARD + h * PIECE, PIECE)]
         each(4, lambda d: push(ZS, block_rows, block_rows, along_z(d), z_recv.at[t]))
         return carry
@@ -188,16 +184,16 @@
     each(8, send_sq)
     keep(SQ, sq_ref.at[:, pl.ds(s * WIDE, WIDE)], sq.at[s])
 
-    send_light(LK, 0, lk_ref, lk, (4, 2))
+    each(8, send_dec)
+    keep(DEC, dec_out.at[group], dec.at[c, rows, :])
+    each(4, lambda d: push(GAIN, gain_out, gains.at[x, z], along_z(d)))
+    keep(GAIN, gain_out, gains.at[x, z])
+    send_light(LK, 0, lk_ref, lk, (2, 4))
     send_light(LV, 0, lv_ref, lv)
-    lax.fori_loop(4, 6, send_z, 0)
-    send_light(LK, 1, lk_ref, lk)
-    send_light(LV, 1, lv_ref, lv)
-    lax.fori_loop(6, 8, send_z, 0)
-    send_light(LQ, 0, lq_ref, lq)
-    send_light(LQ, 1, lq_ref, lq)
-    landed(recv.at[GAIN], gains.at[0])
-    each(4, lambda d: push(GAINS, gains.at[x], gains.at[x], along_x(d)))
+    def pass_gains():
+        landed(recv.at[GAIN], gains.at[0])
+        each(4, lambda d: push(GAINS, gains.at[x], gains.at[x], along_x(d)))
+
 
     def continues(p, carry):
         same = jnp.where(doc_of(p * RUN + RUN - 1) == doc_of(p * RUN - 1), 1.0, 0.0)
@@ -418,28 +414,43 @@
         def at(n, work, *args):
             pl.when(t == n)(lambda: work(*args))
 
-        pl.when(t < 4)(lambda: send_near(t))
-        pl.when((t >= 2) & (t < 5))(lambda: pass_on(t - 2))
-        at(3, prepare)
-        at(3, all_queries)
-        pl.when(t >= 4)(lambda: soft_piece(t - 4))
-        at(4, states, 0)
-        at(4, send_near, 4)
-        at(4, send_near, 5)
-        at(4, pass_on, 3)
-        at(6, states, 1)
-        at(6, send_near, 6)
-        at(7, entering_states, 0)
-        at(7, send_near, 7)
-        pl.when((t >= 6) & (t < 10))(lambda: pass_on(t - 2))
-        at(8, entering_states, 1)
-        at(8, within, 0)
-        at(8, light_outputs, 0)
-        at(9, within, 1)
-        at(9, light_outputs, 1)
+        soft_piece(t)
+        at(0, pass_on, 2)
+        at(0, pass_gains)
+        at(1, pass_on, 3)
+        at(1, states, 0)
+        at(1, send_near, 4)
+        at(1, send_near, 5)
+        at(3, states, 1)
+        at(3, send_near, 6)
+        at(3, pass_on, 4)
+        at(3, entering_states, 0)
+        at(3, send_near, 7)
+        at(3, pass_on, 5)
+        at(4, entering_states, 1)
+        at(4, within, 0)
+        at(4, pass_on, 6)
+        at(4, light_outputs, 0)
+        at(4, pass_on, 7)
         return carry
 
-    lax.fori_loop(0, 12, step, 0)
+    send_near(0)
+    lax.fori_loop(4, 6, send_z, 0)
+    send_light(LK, 1, lk_ref, lk)
+    send_light(LV, 1, lv_ref, lv)
+    lax.fori_loop(6, 8, send_z, 0)
+    send_light(LQ, 0, lq_ref, lq)
+    send_light(LQ, 1, lq_ref, lq)
+    send_near(1)
+    pass_on(0)
+    send_near(2)
+    prepare()
+    pass_on(1)
+    send_near(3)
+    all_queries()
+    lax.fori_loop(0, 8, step, 0)
+    within(1)
+    light_outputs(1)
 
     landed(send.at[KV], kv.at[pl.ds(0, 7 * PIECE)])
     landed(send.at[DEC], dec_out.at[pl.ds(0, 7)])
@@ -502,6 +513,7 @@
         pltpu.SemaphoreType.DMA((8,)),
         pltpu.SemaphoreType.DMA((8,)),
         pltpu.SemaphoreType.DMA((8,)),
+        pltpu.SemaphoreType.DMA((8,)),
     ]
     return pl.pallas_call(
         kernel,

time: 88.1 us -> 86.4 us (0.981); the launches traced: 86.6 us -> 86.2 us
  no operation moved by 1% of the time
where the time goes in v4:
time: 86.4 us; the launch traced here: 86.2 us
  Pallas kernels  82.2 us (95%)
  local copies, waits for them, and re-layouts  3.32 us (4%)
    pallas_call x1, Pallas kernels, per_device(): pl.pallas_call(kernel, out_shape=(out, out), in_specs=[pl.BlockSpec(memor...  82.2 us
    unnamed x4, local copies, waits for them, and re-layouts  3.32 us

profile of v4, /device:TPU:25, one launch (start us, length us, event | category | flops | bytes accessed | tf_op | source)
XLA Modules:
  0.0 86.2 jit_solution(14049057408086298594)
XLA Ops:
  0.6 82.2 %shard_map.95 = (bf16[64,8192]{1,0:T(8,128)(2,1)}, bf16[64,8192]{1,0:T(8,128)(2,1)}) custom-call(s32[8]{0:T(128)} %docs_ref.1, bf16[64,8192]{1,0:T(8,128)(2,1)} %lq_ref.1, bf16[64,8192]{1,0:T(8,128)(2,1)} %lk_ref.1, bf16[64,8192]{1,0:T(8,128)(2,1)} %lv_ref.1, bf16[64,64]{1,0:T(8,128)(2,1)} %dec_ref.1, bf16[4,128]{1,0:T(4,128)(2,1)} %bitcast.1, ...), custom_call_target="tpu_custom_call" | custom-call | tf_op jit(solution)/shard_map/pallas_call | solution.py:518
  82.9 0.0 copy-start
  82.9 2.4 %copy.12 = bf16[64,8192]{1,0:T(8,128)(2,1)} copy(bf16[64,8192]{1,0:T(8,128)(2,1)} %get-tuple-element.4) | data formatting | bytes 2097152
  85.3 0.0 copy-done
  85.3 1.0 %copy.13 = bf16[64,8192]{1,0:T(8,128)(2,1)} copy(bf16[64,8192]{1,0:T(8,128)(2,1)S(1)} %copy-done) | data formatting | bytes 2097152
Async XLA Ops:
  82.9 2.4 %copy-start = (bf16[64,8192]{1,0:T(8,128)(2,1)S(1)}, bf16[64,8192]{1,0:T(8,128)(2,1)}, u32[]{:S(2)}) copy-start(bf16[64,8192]{1,0:T(8,128)(2,1)} %get-tuple-element.5) | copy-start | bytes 3145732

commit v5 on v4

--- a/solution.py
+++ b/solution.py
@@ -422,8 +422,8 @@
         at(1, send_near, 4)
         at(1, send_near, 5)
         at(3, states, 1)
+        at(3, pass_on, 4)
         at(3, send_near, 6)
-        at(3, pass_on, 4)
         at(3, entering_states, 0)
         at(3, send_near, 7)
         at(3, pass_on, 5)

time: 86.4 us -> 85.7 us (level)
  no operation moved by 1% of the time
where the time goes in v5:
time: 85.7 us; the launch traced here: 85.5 us
  Pallas kernels  81.5 us (95%)
  local copies, waits for them, and re-layouts  3.32 us (4%)
    pallas_call x1, Pallas kernels, per_device(): pl.pallas_call(kernel, out_shape=(out, out), in_specs=[pl.BlockSpec(memor...  81.5 us
    unnamed x4, local copies, waits for them, and re-layouts  3.32 us

profile of v5, /device:TPU:25, one launch (start us, length us, event | category | flops | bytes accessed | tf_op | source)
XLA Modules:
  0.0 85.5 jit_solution(16564332243609833939)
XLA Ops:
  0.6 81.5 %shard_map.95 = (bf16[64,8192]{1,0:T(8,128)(2,1)}, bf16[64,8192]{1,0:T(8,128)(2,1)}) custom-call(s32[8]{0:T(128)} %docs_ref.1, bf16[64,8192]{1,0:T(8,128)(2,1)} %lq_ref.1, bf16[64,8192]{1,0:T(8,128)(2,1)} %lk_ref.1, bf16[64,8192]{1,0:T(8,128)(2,1)} %lv_ref.1, bf16[64,64]{1,0:T(8,128)(2,1)} %dec_ref.1, bf16[4,128]{1,0:T(4,128)(2,1)} %bitcast.1, ...), custom_call_target="tpu_custom_call" | custom-call | tf_op jit(solution)/shard_map/pallas_call | solution.py:518
  82.2 0.0 copy-start
  82.2 2.4 %copy.12 = bf16[64,8192]{1,0:T(8,128)(2,1)} copy(bf16[64,8192]{1,0:T(8,128)(2,1)} %get-tuple-element.4) | data formatting | bytes 2097152
  84.5 0.0 copy-done
  84.5 1.0 %copy.13 = bf16[64,8192]{1,0:T(8,128)(2,1)} copy(bf16[64,8192]{1,0:T(8,128)(2,1)S(1)} %copy-done) | data formatting | bytes 2097152
Async XLA Ops:
  82.2 2.4 %copy-start = (bf16[64,8192]{1,0:T(8,128)(2,1)S(1)}, bf16[64,8192]{1,0:T(8,128)(2,1)}, u32[]{:S(2)}) copy-start(bf16[64,8192]{1,0:T(8,128)(2,1)} %get-tuple-element.5) | copy-start | bytes 3145732
